TPU v7x, 32 devices: a whole 2x2x4 slice. The times are simulated.
32 devices in a mesh: groups: 2 (over y), gx: 4 (over z), gy: 2 (over x), gz: 2 (over core).
Axes of the slice: x: 2, y: 2, z: 4, core: 2. Of those that a mesh axis runs over, the one named last changes fastest.
Arguments:
- positions: float32 [3, 8, 2, 64], P(None, ('groups', 'gx'), 'gy'), parts along dimension 1, may hold values from 0 to 20
- species: int32 [8, 2, 64], P(('groups', 'gx'), 'gy'), parts along dimension 0, may hold values from 0 to 4
- centers: int32 [8, 2, 1024], P(('groups', 'gx'), 'gy'), parts along dimension 0, may hold values from 0 to 63
- neighbours: int32 [8, 2, 1024], P(('groups', 'gx'), 'gy'), parts along dimension 0, may hold values from 0 to 223, as said below
- masks: int32 [8, 2, 1024], P(('groups', 'gx'), 'gy'), parts along dimension 0, may hold values from 0 to 1, as said below
- skin: int32 [8, 2, 32], P(('groups', 'gx'), 'gy'), parts along dimension 0, may hold values from 0 to 63, as said below
- embed: float32 [4, 5, 32], P('gz'), may hold values from -6 to 6
- radial: float32 [4, 8, 32], P('gz'), may hold values from -2 to 2
- w_mix: float32 [4, 2, 32, 32], P('gz'), may hold values from -1 to 1
- w_latent: float32 [4, 1, 32, 32], P('gz'), may hold values from -1 to 1
- w_update: float32 [4, 2, 32, 32], P('gz'), may hold values from -1 to 1
- readout: float32 [4, 32], P('gz'), may hold values from -1 to 1
Outputs:
- forces: float32 [4, 3, 8, 2, 64], P('gz', None, ('groups', 'gx'), 'gy'), parts along dimension 2
There are 2 independent parts, one for each index of `groups`. A program takes and returns all parts, laid end to end along the dimension named above; an argument that names none is the same for every part. Nothing has to cross between parts.
Inputs may be any that keep to these rules, and one draw needn't show every extreme that they name: `neighbours`: each value is an own atom (below 64) or an entry of a face or corner slot of the table. `masks`: in each domain the live edge slots fill whole tiles of 128 from the first tile; at least a quarter of the 8 tiles (rounded down) are live, and domain (0, 0) has all 8 live. `skin`: 32 distinct atoms of the domain; the first 8 of them are the list that corner neighbours receive.
All inputs are finite; a program needn't handle non-finite values.
Results may differ from a plain program's by a relative error of at most 0.0003.
Values sent between devices are 32-bit elements; how exact they have to be, the bound alone decides.
No kernel may reach another device: no remote copies, remote signals or barrier semaphores. Data moves between devices by JAX's collectives and lax.ppermute only.
A program may use at most 64 MiB of HBM per device.

v0:
```python
from functools import partial

import jax
import jax.numpy as jnp
from jax import lax
from jax.sharding import PartitionSpec as P

NEIGH = 16


box_edge = 20.0
energy_scale = 16.0
highest = lax.Precision.HIGHEST
face_slots = ((0, 1), (1, 0), (1, 2), (2, 1))
corner_slots = ((0, 0), (0, 2), (2, 0), (2, 2))


def passed_along(value, axis, by):
    peers = lax.axis_size(axis)
    return lax.ppermute(value, axis, [(i, (i + by) % peers) for i in range(peers)])


def padded(cells, sides, width):
    for axis, dim in sides:
        count = lax.axis_size(axis)
        head = lax.slice_in_dim(cells, 0, width, axis=dim)
        tail = lax.slice_in_dim(cells, cells.shape[dim] - width, cells.shape[dim], axis=dim)
        cells = jnp.concatenate(
            [
                lax.ppermute(tail, axis, [(i, (i + 1) % count) for i in range(count)]),
                cells,
                lax.ppermute(head, axis, [((i + 1) % count, i) for i in range(count)]),
            ],
            axis=dim,
        )
    return cells


def slot_offsets(ghost_count, corner_count):
    first_parts = []
    second_parts = []
    for slot_pair in face_slots:
        first_parts.append(jnp.full((ghost_count,), slot_pair[0] - 1.0, jnp.float32))
        second_parts.append(jnp.full((ghost_count,), slot_pair[1] - 1.0, jnp.float32))
    for slot_pair in corner_slots:
        first_parts.append(jnp.full((corner_count,), slot_pair[0] - 1.0, jnp.float32))
        second_parts.append(jnp.full((corner_count,), slot_pair[1] - 1.0, jnp.float32))
    first_row = jnp.concatenate(first_parts)
    return jnp.stack([first_row, jnp.concatenate(second_parts), jnp.zeros_like(first_row)])


def project(weight, values):
    return jnp.einsum("mcd,mce->mde", weight, values, precision=highest)


def pass_corner(rows, direction):
    return passed_along(rows, "gy", direction)


def send_rows(row_block):
    ghost_count = row_block.shape[1]
    corner_count = ghost_count // 4
    spread = row_block[:, None, None, :]
    extended = padded(spread, (("gx", 1), ("gy", 2)), 1)
    lower_x = extended[:, 0, 1]
    upper_x = extended[:, 2, 1]
    pieces = [
        lower_x,
        extended[:, 1, 0],
        extended[:, 1, 2],
        upper_x,
        pass_corner(lower_x[:, :corner_count], 1),
        pass_corner(lower_x[:, :corner_count], -1),
        pass_corner(upper_x[:, :corner_count], 1),
        pass_corner(upper_x[:, :corner_count], -1),
    ]
    return jnp.concatenate(pieces, axis=1)


def pass_x(slot_block, direction):
    return passed_along(slot_block, "gx", direction)


def pass_y(slot_block, direction):
    return passed_along(slot_block, "gy", direction)


def return_rows(slot_grads, ghost_count):
    row_count = slot_grads.shape[0]
    corner_count = ghost_count // 4
    faces = slot_grads[:, : 4 * ghost_count].reshape(row_count, 4, ghost_count)
    corners = slot_grads[:, 4 * ghost_count :].reshape(row_count, 4, corner_count)
    lower_x = (
        faces[:, 0].at[:, :corner_count].add(pass_y(corners[:, 0], -1) + pass_y(corners[:, 1], 1))
    )
    upper_x = (
        faces[:, 3].at[:, :corner_count].add(pass_y(corners[:, 2], -1) + pass_y(corners[:, 3], 1))
    )
    collected = (
        pass_x(lower_x, -1) + pass_x(upper_x, 1) + pass_y(faces[:, 1], -1) + pass_y(faces[:, 2], 1)
    )
    return collected


def geometry(offset_vecs, radial):
    distance = jnp.sqrt(jnp.sum(offset_vecs * offset_vecs, axis=1) + 1.0)
    freqs = jnp.arange(radial.shape[1], dtype=jnp.float32) / 4.0
    basis = (
        jnp.cos(freqs[None, :, None] * distance[:, None, :]) * jnp.exp(-distance / 32.0)[:, None, :]
    )
    return jax.nn.silu(project(radial, basis))


def advance(feature_table, latent, join_hot, center_hot, live_edges, mix_w, update_w, latent_w):
    joined = jnp.einsum("mcs,se->mce", feature_table, join_hot, precision=highest)
    activated = jax.nn.silu(project(mix_w, latent * joined)) * live_edges[None, None, :]
    summed = jnp.einsum("mce,ae->mca", activated, center_hot, precision=highest)
    atom_count = center_hot.shape[0]
    features = feature_table[:, :, :atom_count] + project(update_w, summed) / NEIGH
    if latent_w is None:
        return features
    return (features, latent + project(latent_w, activated))


def on_device(
    positions,
    species,
    centers,
    neighbours,
    masks,
    skin,
    embed,
    radial,
    w_mix,
    w_latent,
    w_update,
    readout,
):
    atom_count = positions.shape[-1]
    member_count, elements, channels = embed.shape
    layer_count = w_mix.shape[1]
    own_pos = positions.reshape(3, atom_count)
    center_idx = centers.reshape(-1)
    neighbour_idx = neighbours.reshape(-1)
    live_edges = masks.reshape(-1).astype(jnp.float32)
    send_list = skin.reshape(-1)
    ghost_count = send_list.shape[0]
    table_ghosts = 4 * ghost_count + ghost_count
    slot_count = atom_count + table_ghosts
    slot_ids = jnp.arange(slot_count, dtype=jnp.int32)[:, None]
    center_slots = (center_idx[None, :] == slot_ids).astype(jnp.float32)
    neighbour_slots = (neighbour_idx[None, :] == slot_ids).astype(jnp.float32)
    join_hot = center_slots + neighbour_slots
    diff_hot = neighbour_slots - center_slots
    center_hot = center_slots[:atom_count]
    one_hot = (species.reshape(1, atom_count) == jnp.arange(elements)[:, None]).astype(jnp.float32)
    features = jnp.einsum("msc,sa->mca", embed, one_hot, precision=highest)
    feature_rows = member_count * channels
    outgoing = jnp.concatenate([features.reshape(feature_rows, atom_count), own_pos], axis=0)[
        :, send_list
    ]
    arrived = send_rows(outgoing)
    ghost_pos = arrived[feature_rows:] + box_edge * slot_offsets(ghost_count, ghost_count // 4)
    pos_table = jnp.concatenate([own_pos, ghost_pos], axis=1)
    offset_vec = jnp.dot(pos_table, diff_hot, precision=highest, preferred_element_type=jnp.float32)
    offset_vecs = jnp.broadcast_to(offset_vec, (member_count,) + offset_vec.shape)
    latent, geometry_back = jax.vjp(lambda vectors: geometry(vectors, radial), offset_vecs)
    feature_table = jnp.concatenate(
        [features, arrived[:feature_rows].reshape(member_count, channels, table_ghosts)], axis=2
    )
    pullbacks = []
    for layer_idx in range(layer_count):
        if layer_idx > 0:
            flat_rows = features.reshape(feature_rows, atom_count)[:, send_list]
            ghost_block = send_rows(flat_rows).reshape(member_count, channels, table_ghosts)
            feature_table = jnp.concatenate([features, ghost_block], axis=2)
        latent_w = w_latent[:, layer_idx] if layer_idx < layer_count - 1 else None
        stepper = partial(
            advance,
            join_hot=join_hot,
            center_hot=center_hot,
            live_edges=live_edges,
            mix_w=w_mix[:, layer_idx],
            update_w=w_update[:, layer_idx],
            latent_w=latent_w,
        )
        if layer_idx == 0:
            fixed_table = feature_table
            outputs, pullback = jax.vjp(lambda latent_in: stepper(fixed_table, latent_in), latent)
        else:
            outputs, pullback = jax.vjp(stepper, feature_table, latent)
        pullbacks.append(pullback)
        if latent_w is None:
            features = outputs
        else:
            features, latent = outputs
    feature_grad = jnp.broadcast_to(energy_scale * readout[:, :, None], features.shape)
    latent_grad = None
    for layer_idx in reversed(range(layer_count)):
        cotangent = feature_grad if latent_grad is None else (feature_grad, latent_grad)
        pulled = pullbacks[layer_idx](cotangent)
        if layer_idx == 0:
            latent_grad = pulled[0]
        else:
            table_grad, latent_grad = pulled
            back_rows = return_rows(
                table_grad[:, :, atom_count:].reshape(feature_rows, table_ghosts), ghost_count
            )
            feature_grad = (
                table_grad[:, :, :atom_count]
                .at[:, :, send_list]
                .add(back_rows.reshape(member_count, channels, ghost_count))
            )
    vector_grad = geometry_back(latent_grad)[0]
    pos_grad = jnp.einsum("mke,se->mks", vector_grad, diff_hot, precision=highest)
    pos_back = return_rows(
        pos_grad[:, :, atom_count:].reshape(member_count * 3, table_ghosts), ghost_count
    )
    own_grad = (
        pos_grad[:, :, :atom_count]
        .at[:, :, send_list]
        .add(pos_back.reshape(member_count, 3, ghost_count))
    )
    return (-own_grad).reshape(member_count, 3, 1, 1, atom_count)


def solution(mesh):
    return jax.shard_map(
        on_device,
        mesh=mesh,
        in_specs=(
            P(None, ("groups", "gx"), "gy", None),
            P(("groups", "gx"), "gy", None),
            P(("groups", "gx"), "gy", None),
            P(("groups", "gx"), "gy", None),
            P(("groups", "gx"), "gy", None),
            P(("groups", "gx"), "gy", None),
            P("gz", None, None),
            P("gz", None, None),
            P("gz", None, None, None),
            P("gz", None, None, None),
            P("gz", None, None, None),
            P("gz", None),
        ),
        out_specs=P("gz", None, ("groups", "gx"), "gy", None),
        check_vma=False,
    )
```

profile of v0, /device:TPU:0, one launch (start us, length us, event | category | flops | bytes accessed | tf_op | source)
XLA Modules:
  0.0 80.4 jit_solution(15596822420524933013)
XLA Ops:
  0.0 0.8 copy.166
  0.8 0.6 copy-done.12
  1.8 0.6 copy-done.13
  2.4 0.6 gather_fusion
  3.1 3.1 %collective-permute-start = (f32[67,1,1,32]{3,0,2,1:T(8,128)S(1)}, f32[67,1,1,32]{3,0,2,1:T(8,128)S(1)}, u32[]{:S(2)}, u32[]{:S(2)}) collective-permute-start(f32[67,1,1,32]{3,0,2,1:T(8,128)S(1)} %bitcast.200), channel_id=1, source_target_pairs={{0,4},{4,8},{8,12},{12,0},{1,5},{5,9},{9,13},{13,1},{2,6},{6,10},{... | collective-permute-start | bytes 25736 | tf_op jit(solution)/shard_map/ppermute | solution.py:30
  6.2 2.1 %collective-permute-start.1 = (f32[67,1,1,32]{3,0,2,1:T(8,128)S(1)}, f32[67,1,1,32]{3,0,2,1:T(8,128)S(1)}, u32[]{:S(2)}, u32[]{:S(2)}) collective-permute-start(f32[67,1,1,32]{3,0,2,1:T(8,128)S(1)} %bitcast.201), channel_id=1, source_target_pairs={{4,0},{8,4},{12,8},{0,12},{5,1},{9,5},{13,9},{1,13},{6,2},{10,6},{... | collective-permute-start | bytes 25736 | tf_op jit(solution)/shard_map/ppermute | solution.py:32
  8.4 0.7 copy-done.2
  9.7 0.6 collective-permute-done
  10.6 1.6 %collective-permute-start.2 = (f32[67,3,1,32]{3,0,2,1:T(8,128)S(1)}, f32[67,3,1,32]{3,0,2,1:T(8,128)S(1)}, u32[]{:S(2)}, u32[]{:S(2)}) collective-permute-start(f32[67,3,1,32]{3,0,2,1:T(8,128)S(1)} %pad_maximum_fusion), channel_id=1, source_target_pairs={{0,2},{2,0},{1,3},{3,1},{4,6},{6,4},{5,7},{7,5},{8,10},{10,8},{9,1... | collective-permute-start | bytes 77192 | tf_op jit(solution)/shard_map/ppermute | solution.py:30
  12.2 0.5 collective-permute-start.3
  12.7 1.5 %collective-permute-start.4 = (f32[67,8]{1,0:T(8,128)S(1)}, f32[67,8]{1,0:T(8,128)S(1)}, u32[]{:S(2)}, u32[]{:S(2)}) collective-permute-start(f32[67,8]{1,0:T(8,128)S(1)} %bitcast.196), channel_id=1, source_target_pairs={{0,2},{2,0},{1,3},{3,1},{4,6},{6,4},{5,7},{7,5},{8,10},{10,8},{9,1... | collective-permute-start | bytes 6440 | tf_op jit(solution)/shard_map/ppermute | solution.py:20
  14.2 0.5 collective-permute-start.5
  14.8 1.6 %collective-permute-done.2 = f32[67,3,1,32]{3,0,2,1:T(8,128)S(1)} collective-permute-done((f32[67,3,1,32]{3,0,2,1:T(8,128)S(1)}, f32[67,3,1,32]{3,0,2,1:T(8,128)S(1)}, u32[]{:S(2)}, u32[]{:S(2)}) %collective-permute-start.2) | collective-permute-done | bytes 25760 | tf_op jit(solution)/shard_map/ppermute | solution.py:30
  16.4 1.2 %collective-permute-done.3 = f32[67,3,1,32]{3,0,2,1:T(8,128)S(1)} collective-permute-done((f32[67,3,1,32]{3,0,2,1:T(8,128)S(1)}, f32[67,3,1,32]{3,0,2,1:T(8,128)S(1)}, u32[]{:S(2)}, u32[]{:S(2)}) %collective-permute-start.3) | collective-permute-done | bytes 25760 | tf_op jit(solution)/shard_map/ppermute | solution.py:32
  18.5 0.6 copy-done.1
  19.2 0.7 copy-done.11
  19.9 0.7 multiply_reduce_fusion
  20.7 0.9 %fusion.15 = f32[2,32,1024]{2,1,0:T(8,128)S(1)} fusion(s32[1024]{0:T(1024)S(1)} %bitcast.223, s32[1024]{0:T(1024)S(1)} %bitcast.236, f32[2,32,160]{2,1,0:T(8,128)S(1)} %bitcast.193, f32[2,32,64]{2,1,0:T(8,128)S(1)} %bitcast.208), kind=kOutput, calls=%fused_computation.30 | convolution fusion | flops 177321984 | bytes 327680 | tf_op jit(solution)/shard_map/jvp(mcs,se->mce)/dot_general | solution.py:115
  21.6 0.5 convolution_bitcast_fusion.6
  22.5 0.5 convolution_bitcast_fusion.5
  23.6 0.6 gather_fusion.1
  24.2 1.1 %collective-permute-start.6 = (f32[64,1,1,32]{0,3,2,1:T(8,128)S(1)}, f32[64,1,1,32]{0,3,2,1:T(8,128)S(1)}, u32[]{:S(2)}, u32[]{:S(2)}) collective-permute-start(f32[64,1,1,32]{0,3,2,1:T(8,128)S(1)} %bitcast.203), channel_id=1, source_target_pairs={{0,4},{4,8},{8,12},{12,0},{1,5},{5,9},{9,13},{13,1},{2,6},{6,10},{... | collective-permute-start | bytes 24584 | tf_op jit(solution)/shard_map/ppermute | solution.py:30
  25.3 2.8 %collective-permute-start.7 = (f32[64,1,1,32]{0,3,2,1:T(8,128)S(1)}, f32[64,1,1,32]{0,3,2,1:T(8,128)S(1)}, u32[]{:S(2)}, u32[]{:S(2)}) collective-permute-start(f32[64,1,1,32]{0,3,2,1:T(8,128)S(1)} %bitcast.204), channel_id=1, source_target_pairs={{4,0},{8,4},{12,8},{0,12},{5,1},{9,5},{13,9},{1,13},{6,2},{10,6},{... | collective-permute-start | bytes 24584 | tf_op jit(solution)/shard_map/ppermute | solution.py:32
  28.1 0.6 compare_reduce_fusion
  28.7 1.1 %collective-permute-done.6 = f32[64,1,1,32]{0,3,2,1:T(8,128)S(1)} collective-permute-done((f32[64,1,1,32]{0,3,2,1:T(8,128)S(1)}, f32[64,1,1,32]{0,3,2,1:T(8,128)S(1)}, u32[]{:S(2)}, u32[]{:S(2)}) %collective-permute-start.6) | collective-permute-done | bytes 8224 | tf_op jit(solution)/shard_map/ppermute | solution.py:30
  29.8 1.4 %collective-permute-start.8 = (f32[64,3,1,32]{0,3,2,1:T(8,128)S(1)}, f32[64,3,1,32]{0,3,2,1:T(8,128)S(1)}, u32[]{:S(2)}, u32[]{:S(2)}) collective-permute-start(f32[64,3,1,32]{0,3,2,1:T(8,128)S(1)} %pad_maximum_fusion.1), channel_id=1, source_target_pairs={{0,2},{2,0},{1,3},{3,1},{4,6},{6,4},{5,7},{7,5},{8,10},{10,8},{9,1... | collective-permute-start | bytes 73736 | tf_op jit(solution)/shard_map/ppermute | solution.py:30
  31.2 0.7 collective-permute-start.9
  31.9 1.4 %collective-permute-start.10 = (f32[64,8]{0,1:T(8,128)S(1)}, f32[64,8]{0,1:T(8,128)S(1)}, u32[]{:S(2)}, u32[]{:S(2)}) collective-permute-start(f32[64,8]{0,1:T(8,128)S(1)} %slice.257), channel_id=1, source_target_pairs={{0,2},{2,0},{1,3},{3,1},{4,6},{6,4},{5,7},{7,5},{8,10},{10,8},{9,1... | collective-permute-start | bytes 6152 | tf_op jit(solution)/shard_map/ppermute | solution.py:20
  33.3 0.7 collective-permute-start.11
  33.9 0.5 fusion.4
  34.5 1.0 %collective-permute-done.10 = f32[64,8]{0,1:T(8,128)S(1)} collective-permute-done((f32[64,8]{0,1:T(8,128)S(1)}, f32[64,8]{0,1:T(8,128)S(1)}, u32[]{:S(2)}, u32[]{:S(2)}) %collective-permute-start.10) | collective-permute-done | bytes 2080 | tf_op jit(solution)/shard_map/ppermute | solution.py:20
  35.6 1.3 %collective-permute-done.11 = f32[64,8]{0,1:T(8,128)S(1)} collective-permute-done((f32[64,8]{0,1:T(8,128)S(1)}, f32[64,8]{0,1:T(8,128)S(1)}, u32[]{:S(2)}, u32[]{:S(2)}) %collective-permute-start.11) | collective-permute-done | bytes 2080 | tf_op jit(solution)/shard_map/ppermute | solution.py:20
  37.3 0.9 %fusion.13 = f32[2,32,1024]{2,1,0:T(8,128)S(1)} fusion(f32[2,32,224]{2,1,0:T(8,128)S(1)} %concatenate.56, s32[1024]{0:T(1024)S(1)} %bitcast.224, s32[1024]{0:T(1024)S(1)} %bitcast.237), kind=kOutput, calls=%fused_computation.29 | convolution fusion | flops 177307648 | bytes 327680 | tf_op jit(solution)/shard_map/jvp(mcs,se->mce)/dot_general | solution.py:115
  38.2 0.4 convolution_bitcast_fusion.3
  38.6 0.5 convolution_bitcast_fusion.2
  39.1 1.0 %convolution_add_fusion = f32[2,32,224]{2,1,0:T(8,128)S(1)} fusion(s32[1024]{0:T(1024)S(1)} %bitcast.225, s32[1024]{0:T(1024)S(1)} %bitcast.238, f32[2,32,1024]{2,1,0:T(8,128)S(1)} %fusion.4, f32[2,32,1024]{2,1,0:T(8,128)S(1)} %convolution_bitcast_fusion.2, f32[2,32,64]{2,1,0:T(8,128)S(1)} %broadcast_in_dim.16), kind=kOutput, calls=%fused_computation.20 | convolution fusion | flops 177387520 | bytes 606208 | tf_op jit(solution)/shard_map/transpose(jvp(mcs,se->mce))/dot_general | solution.py:115
  40.5 0.7 collective-permute-start.15
  41.1 1.4 %collective-permute-start.16 = (f32[64,8]{0,1:T(8,128)S(1)}, f32[64,8]{0,1:T(8,128)S(1)}, u32[]{:S(2)}, u32[]{:S(2)}) collective-permute-start(f32[64,8]{0,1:T(8,128)S(1)} %get-tuple-element.63), channel_id=1, source_target_pairs={{0,2},{2,0},{1,3},{3,1},{4,6},{6,4},{5,7},{7,5},{8,10},{10,8},{9,1... | collective-permute-start | bytes 6152 | tf_op jit(solution)/shard_map/ppermute | solution.py:20
  42.5 0.7 collective-permute-start.12
  43.2 1.4 %collective-permute-start.13 = (f32[64,8]{0,1:T(8,128)S(1)}, f32[64,8]{0,1:T(8,128)S(1)}, u32[]{:S(2)}, u32[]{:S(2)}) collective-permute-start(f32[64,8]{0,1:T(8,128)S(1)} %get-tuple-element.65), channel_id=1, source_target_pairs={{0,2},{2,0},{1,3},{3,1},{4,6},{6,4},{5,7},{7,5},{8,10},{10,8},{9,1... | collective-permute-start | bytes 6152 | tf_op jit(solution)/shard_map/ppermute | solution.py:20
  44.5 0.7 collective-permute-start.19
  45.2 1.4 %collective-permute-start.18 = (f32[64,32]{0,1:T(8,128)S(1)}, f32[64,32]{0,1:T(8,128)S(1)}, u32[]{:S(2)}, u32[]{:S(2)}) collective-permute-start(f32[64,32]{0,1:T(8,128)S(1)} %get-tuple-element.59), channel_id=1, source_target_pairs={{0,2},{2,0},{1,3},{3,1},{4,6},{6,4},{5,7},{7,5},{8,10},{10,8},{9,1... | collective-permute-start | bytes 24584 | tf_op jit(solution)/shard_map/ppermute | solution.py:20
  46.8 0.7 fusion.96
  47.4 3.9 %collective-permute-start.14 = (f32[64,32]{0,1:T(8,128)S(1)}, f32[64,32]{0,1:T(8,128)S(1)}, u32[]{:S(2)}, u32[]{:S(2)}) collective-permute-start(f32[64,32]{0,1:T(8,128)S(1)} %get-tuple-element.56), channel_id=1, source_target_pairs={{0,12},{4,0},{8,4},{12,8},{1,13},{5,1},{9,5},{13,9},{2,14},{6,2},{... | collective-permute-start | bytes 24584 | tf_op jit(solution)/shard_map/ppermute | solution.py:20
  51.4 1.3 %collective-permute-done.14 = f32[64,32]{0,1:T(8,128)S(1)} collective-permute-done((f32[64,32]{0,1:T(8,128)S(1)}, f32[64,32]{0,1:T(8,128)S(1)}, u32[]{:S(2)}, u32[]{:S(2)}) %collective-permute-start.14) | collective-permute-done | bytes 8224 | tf_op jit(solution)/shard_map/ppermute | solution.py:20
  52.7 4.1 %collective-permute-done.17 = f32[64,32]{0,1:T(8,128)S(1)} collective-permute-done((f32[64,32]{0,1:T(8,128)S(1)}, f32[64,32]{0,1:T(8,128)S(1)}, u32[]{:S(2)}, u32[]{:S(2)}) %collective-permute-start.17) | collective-permute-done | bytes 8224 | tf_op jit(solution)/shard_map/ppermute | solution.py:20
  56.9 1.6 %scatter_fusion = f32[2,32,64]{1,0,2:T(2,128)S(1)} fusion(f32[2,32,64]{1,0,2:T(2,128)S(1)} %copy.186, s32[32]{0:T(128)S(1)} %fusion.103, f32[32,2,32]{2,1,0:T(2,128)S(1)} %bitcast.206), kind=kCustom, calls=%fused_computation.2 | custom fusion | flops 2048 | bytes 24704 | tf_op jit(solution)/shard_map/scatter-add | solution.py:212
  59.5 0.5 fusion.1
  60.4 1.0 %fusion.9 = f32[2,3,224]{2,1,0:T(4,128)S(1)} fusion(s32[1024]{0:T(1024)S(1)} %bitcast.226, s32[1024]{0:T(1024)S(1)} %bitcast.239, f32[3,1024]{1,0:T(4,128)S(1)} %get-tuple-element.62, f32[2,1024]{1,0:T(2,128)S(1)} %add_multiply_fusion), kind=kOutput, calls=%fused_computation.27 | convolution fusion | flops 17668096 | bytes 34048 | tf_op jit(solution)/shard_map/mke,se->mks/dot_general | solution.py:215
  61.7 0.5 copy-done.3
  62.1 1.4 %collective-permute-start.27 = (f32[6,32]{1,0:T(8,128)S(1)}, f32[6,32]{1,0:T(8,128)S(1)}, u32[]{:S(2)}, u32[]{:S(2)}) collective-permute-start(f32[6,32]{1,0:T(8,128)S(1)} %bitcast.227), channel_id=1, source_target_pairs={{0,2},{2,0},{1,3},{3,1},{4,6},{6,4},{5,7},{7,5},{8,10},{10,8},{9,1... | collective-permute-start | bytes 2312 | tf_op jit(solution)/shard_map/ppermute | solution.py:20
  63.5 0.6 collective-permute-start.26
  64.3 1.4 %collective-permute-start.20 = (f32[6,8]{1,0:T(8,128)S(1)}, f32[6,8]{1,0:T(8,128)S(1)}, u32[]{:S(2)}, u32[]{:S(2)}) collective-permute-start(f32[6,8]{1,0:T(8,128)S(1)} %bitcast.234), channel_id=1, source_target_pairs={{0,2},{2,0},{1,3},{3,1},{4,6},{6,4},{5,7},{7,5},{8,10},{10,8},{9,1... | collective-permute-start | bytes 584 | tf_op jit(solution)/shard_map/ppermute | solution.py:20
  65.7 0.7 collective-permute-start.21
  66.4 1.4 %collective-permute-start.23 = (f32[6,8]{1,0:T(8,128)S(1)}, f32[6,8]{1,0:T(8,128)S(1)}, u32[]{:S(2)}, u32[]{:S(2)}) collective-permute-start(f32[6,8]{1,0:T(8,128)S(1)} %bitcast.231), channel_id=1, source_target_pairs={{0,2},{2,0},{1,3},{3,1},{4,6},{6,4},{5,7},{7,5},{8,10},{10,8},{9,1... | collective-permute-start | bytes 584 | tf_op jit(solution)/shard_map/ppermute | solution.py:20
  68.0 1.4 %collective-permute-start.24 = (f32[6,8]{1,0:T(8,128)S(1)}, f32[6,8]{1,0:T(8,128)S(1)}, u32[]{:S(2)}, u32[]{:S(2)}) collective-permute-start(f32[6,8]{1,0:T(8,128)S(1)} %bitcast.232), channel_id=1, source_target_pairs={{0,2},{2,0},{1,3},{3,1},{4,6},{6,4},{5,7},{7,5},{8,10},{10,8},{9,1... | collective-permute-start | bytes 584 | tf_op jit(solution)/shard_map/ppermute | solution.py:20
  69.3 0.7 add_select_fusion.1
  70.3 1.3 %collective-permute-done.24 = f32[6,8]{1,0:T(8,128)S(1)} collective-permute-done((f32[6,8]{1,0:T(8,128)S(1)}, f32[6,8]{1,0:T(8,128)S(1)}, u32[]{:S(2)}, u32[]{:S(2)}) %collective-permute-start.24) | collective-permute-done | bytes 224 | tf_op jit(solution)/shard_map/ppermute | solution.py:20
  71.6 0.7 add_select_fusion
  72.4 0.8 collective-permute-start.25
  73.3 0.5 collective-permute-done.22
  73.9 4.0 %collective-permute-done.25 = f32[6,32]{1,0:T(8,128)S(1)} collective-permute-done((f32[6,32]{1,0:T(8,128)S(1)}, f32[6,32]{1,0:T(8,128)S(1)}, u32[]{:S(2)}, u32[]{:S(2)}) %collective-permute-start.25) | collective-permute-done | bytes 800 | tf_op jit(solution)/shard_map/ppermute | solution.py:20
  78.0 1.6 %scatter_fusion.1 = f32[2,3,64]{1,0,2:T(2,128)S(1)} fusion(f32[2,3,64]{1,0,2:T(2,128)S(1)} %copy.193, s32[32]{0:T(128)S(1)} %fusion.103, f32[32,2,3]{2,1,0:T(2,128)S(1)} %copy.194), kind=kCustom, calls=%fused_computation.3 | custom fusion | flops 192 | bytes 2432 | tf_op jit(solution)/shard_map/scatter-add | solution.py:222
  79.7 0.7 copy.195
  (121 shorter events, 7.6 us)
Async XLA Ops:
  0.0 33.9 %copy-start = (f32[2,1,32,32]{3,2,1,0:T(8,128)S(1)}, f32[2,1,32,32]{3,2,1,0:T(8,128)}, u32[]{:S(2)}) copy-start(f32[2,1,32,32]{3,2,1,0:T(8,128)} %param.29) | copy-start | bytes 24580
  0.0 0.8 copy-start.10
  0.8 0.7 copy-start.12
  1.7 0.7 copy-start.13
  3.0 5.3 %copy-start.9 = (s32[1,1,1024]{2,1,0:T(1,128)S(1)}, s32[1,1,1024]{2,1,0:T(1,128)}, u32[]{:S(2)}) copy-start(s32[1,1,1024]{2,1,0:T(1,128)} %param.24) | copy-start | bytes 12292
  3.1 5.2 %copy-start.6 = (s32[1,1,1024]{2,1,0:T(1,128)S(1)}, s32[1,1,1024]{2,1,0:T(1,128)}, u32[]{:S(2)}) copy-start(s32[1,1,1024]{2,1,0:T(1,128)} %param.22) | copy-start | bytes 12292
  3.1 7.1 %collective-permute-start = (f32[67,1,1,32]{3,0,2,1:T(8,128)S(1)}, f32[67,1,1,32]{3,0,2,1:T(8,128)S(1)}, u32[]{:S(2)}, u32[]{:S(2)}) collective-permute-start(f32[67,1,1,32]{3,0,2,1:T(8,128)S(1)} %bitcast.200), channel_id=1, source_target_pairs={{0,4},{4,8},{8,12},{12,0},{1,5},{5,9},{9,13},{13,1},{2,6},{6,10},{... | collective-permute-start | bytes 25736 | tf_op jit(solution)/shard_map/ppermute | solution.py:30
  6.2 4.4 %collective-permute-start.1 = (f32[67,1,1,32]{3,0,2,1:T(8,128)S(1)}, f32[67,1,1,32]{3,0,2,1:T(8,128)S(1)}, u32[]{:S(2)}, u32[]{:S(2)}) collective-permute-start(f32[67,1,1,32]{3,0,2,1:T(8,128)S(1)} %bitcast.201), channel_id=1, source_target_pairs={{4,0},{8,4},{12,8},{0,12},{5,1},{9,5},{13,9},{1,13},{6,2},{10,6},{... | collective-permute-start | bytes 25736 | tf_op jit(solution)/shard_map/ppermute | solution.py:32
  8.3 0.8 %copy-start.2 = (f32[2,2,32,32]{3,2,1,0:T(8,128)S(1)}, f32[2,2,32,32]{3,2,1,0:T(8,128)}, u32[]{:S(2)}) copy-start(f32[2,2,32,32]{3,2,1,0:T(8,128)} %param.30) | copy-start | bytes 49156
  8.3 0.8 %copy-start.7 = (f32[2,32]{1,0:T(2,128)S(1)}, f32[2,32]{1,0:T(2,128)}, u32[]{:S(2)}) copy-start(f32[2,32]{1,0:T(2,128)} %param.31) | copy-start | bytes 772
  10.6 5.8 %collective-permute-start.2 = (f32[67,3,1,32]{3,0,2,1:T(8,128)S(1)}, f32[67,3,1,32]{3,0,2,1:T(8,128)S(1)}, u32[]{:S(2)}, u32[]{:S(2)}) collective-permute-start(f32[67,3,1,32]{3,0,2,1:T(8,128)S(1)} %pad_maximum_fusion), channel_id=1, source_target_pairs={{0,2},{2,0},{1,3},{3,1},{4,6},{6,4},{5,7},{7,5},{8,10},{10,8},{9,1... | collective-permute-start | bytes 77192 | tf_op jit(solution)/shard_map/ppermute | solution.py:30
  12.2 5.4 %collective-permute-start.3 = (f32[67,3,1,32]{3,0,2,1:T(8,128)S(1)}, f32[67,3,1,32]{3,0,2,1:T(8,128)S(1)}, u32[]{:S(2)}, u32[]{:S(2)}) collective-permute-start(f32[67,3,1,32]{3,0,2,1:T(8,128)S(1)} %pad_maximum_fusion), channel_id=1, source_target_pairs={{2,0},{0,2},{3,1},{1,3},{6,4},{4,6},{7,5},{5,7},{10,8},{8,10},{11,... | collective-permute-start | bytes 77192 | tf_op jit(solution)/shard_map/ppermute | solution.py:32
  12.7 5.2 %collective-permute-start.4 = (f32[67,8]{1,0:T(8,128)S(1)}, f32[67,8]{1,0:T(8,128)S(1)}, u32[]{:S(2)}, u32[]{:S(2)}) collective-permute-start(f32[67,8]{1,0:T(8,128)S(1)} %bitcast.196), channel_id=1, source_target_pairs={{0,2},{2,0},{1,3},{3,1},{4,6},{6,4},{5,7},{7,5},{8,10},{10,8},{9,1... | collective-permute-start | bytes 6440 | tf_op jit(solution)/shard_map/ppermute | solution.py:20
  14.2 4.1 %collective-permute-start.5 = (f32[67,8]{1,0:T(8,128)S(1)}, f32[67,8]{1,0:T(8,128)S(1)}, u32[]{:S(2)}, u32[]{:S(2)}) collective-permute-start(f32[67,8]{1,0:T(8,128)S(1)} %bitcast.198), channel_id=1, source_target_pairs={{0,2},{2,0},{1,3},{3,1},{4,6},{6,4},{5,7},{7,5},{8,10},{10,8},{9,1... | collective-permute-start | bytes 6440 | tf_op jit(solution)/shard_map/ppermute | solution.py:20
  18.5 0.6 copy-start.1
  18.5 0.7 copy-start.8
  19.2 0.7 copy-start.11
  19.9 0.8 %slice-start = ((f32[67,160]{1,0:T(8,128)}), f32[64,160]{1,0:T(8,128)S(1)}, s32[]{:S(2)}) async-start(f32[67,160]{1,0:T(8,128)} %copy-done.1), calls=%async_computation | async-start | bytes 131072 | tf_op jit(solution)/shard_map/slice | solution.py:169
  20.7 0.9 %copy-start.5 = (f32[2,8,32]{2,1,0:T(8,128)S(1)}, f32[2,8,32]{2,1,0:T(8,128)}, u32[]{:S(2)}) copy-start(f32[2,8,32]{2,1,0:T(8,128)} %param.27) | copy-start | bytes 6148
  21.6 0.8 %copy-start.4 = (f32[2,2,32,32]{3,2,1,0:T(8,128)S(1)}, f32[2,2,32,32]{3,2,1,0:T(8,128)}, u32[]{:S(2)}) copy-start(f32[2,2,32,32]{3,2,1,0:T(8,128)} %param.28) | copy-start | bytes 49156
  24.2 5.6 %collective-permute-start.6 = (f32[64,1,1,32]{0,3,2,1:T(8,128)S(1)}, f32[64,1,1,32]{0,3,2,1:T(8,128)S(1)}, u32[]{:S(2)}, u32[]{:S(2)}) collective-permute-start(f32[64,1,1,32]{0,3,2,1:T(8,128)S(1)} %bitcast.203), channel_id=1, source_target_pairs={{0,4},{4,8},{8,12},{12,0},{1,5},{5,9},{9,13},{13,1},{2,6},{6,10},{... | collective-permute-start | bytes 24584 | tf_op jit(solution)/shard_map/ppermute | solution.py:30
  25.3 4.5 %collective-permute-start.7 = (f32[64,1,1,32]{0,3,2,1:T(8,128)S(1)}, f32[64,1,1,32]{0,3,2,1:T(8,128)S(1)}, u32[]{:S(2)}, u32[]{:S(2)}) collective-permute-start(f32[64,1,1,32]{0,3,2,1:T(8,128)S(1)} %bitcast.204), channel_id=1, source_target_pairs={{4,0},{8,4},{12,8},{0,12},{5,1},{9,5},{13,9},{1,13},{6,2},{10,6},{... | collective-permute-start | bytes 24584 | tf_op jit(solution)/shard_map/ppermute | solution.py:32
  29.8 7.2 %collective-permute-start.8 = (f32[64,3,1,32]{0,3,2,1:T(8,128)S(1)}, f32[64,3,1,32]{0,3,2,1:T(8,128)S(1)}, u32[]{:S(2)}, u32[]{:S(2)}) collective-permute-start(f32[64,3,1,32]{0,3,2,1:T(8,128)S(1)} %pad_maximum_fusion.1), channel_id=1, source_target_pairs={{0,2},{2,0},{1,3},{3,1},{4,6},{6,4},{5,7},{7,5},{8,10},{10,8},{9,1... | collective-permute-start | bytes 73736 | tf_op jit(solution)/shard_map/ppermute | solution.py:30
  31.2 5.8 %collective-permute-start.9 = (f32[64,3,1,32]{0,3,2,1:T(8,128)S(1)}, f32[64,3,1,32]{0,3,2,1:T(8,128)S(1)}, u32[]{:S(2)}, u32[]{:S(2)}) collective-permute-start(f32[64,3,1,32]{0,3,2,1:T(8,128)S(1)} %pad_maximum_fusion.1), channel_id=1, source_target_pairs={{2,0},{0,2},{3,1},{1,3},{6,4},{4,6},{7,5},{5,7},{10,8},{8,10},{11,... | collective-permute-start | bytes 73736 | tf_op jit(solution)/shard_map/ppermute | solution.py:32
  31.9 3.6 %collective-permute-start.10 = (f32[64,8]{0,1:T(8,128)S(1)}, f32[64,8]{0,1:T(8,128)S(1)}, u32[]{:S(2)}, u32[]{:S(2)}) collective-permute-start(f32[64,8]{0,1:T(8,128)S(1)} %slice.257), channel_id=1, source_target_pairs={{0,2},{2,0},{1,3},{3,1},{4,6},{6,4},{5,7},{7,5},{8,10},{10,8},{9,1... | collective-permute-start | bytes 6152 | tf_op jit(solution)/shard_map/ppermute | solution.py:20
  33.3 3.6 %collective-permute-start.11 = (f32[64,8]{0,1:T(8,128)S(1)}, f32[64,8]{0,1:T(8,128)S(1)}, u32[]{:S(2)}, u32[]{:S(2)}) collective-permute-start(f32[64,8]{0,1:T(8,128)S(1)} %slice.258), channel_id=1, source_target_pairs={{0,2},{2,0},{1,3},{3,1},{4,6},{6,4},{5,7},{7,5},{8,10},{10,8},{9,1... | collective-permute-start | bytes 6152 | tf_op jit(solution)/shard_map/ppermute | solution.py:20
  40.5 4.7 %collective-permute-start.15 = (f32[64,8]{0,1:T(8,128)S(1)}, f32[64,8]{0,1:T(8,128)S(1)}, u32[]{:S(2)}, u32[]{:S(2)}) collective-permute-start(f32[64,8]{0,1:T(8,128)S(1)} %get-tuple-element.64), channel_id=1, source_target_pairs={{0,2},{2,0},{1,3},{3,1},{4,6},{6,4},{5,7},{7,5},{8,10},{10,8},{9,1... | collective-permute-start | bytes 6152 | tf_op jit(solution)/shard_map/ppermute | solution.py:20
  41.1 5.4 %collective-permute-start.16 = (f32[64,8]{0,1:T(8,128)S(1)}, f32[64,8]{0,1:T(8,128)S(1)}, u32[]{:S(2)}, u32[]{:S(2)}) collective-permute-start(f32[64,8]{0,1:T(8,128)S(1)} %get-tuple-element.63), channel_id=1, source_target_pairs={{0,2},{2,0},{1,3},{3,1},{4,6},{6,4},{5,7},{7,5},{8,10},{10,8},{9,1... | collective-permute-start | bytes 6152 | tf_op jit(solution)/shard_map/ppermute | solution.py:20
  42.5 4.1 %collective-permute-start.12 = (f32[64,8]{0,1:T(8,128)S(1)}, f32[64,8]{0,1:T(8,128)S(1)}, u32[]{:S(2)}, u32[]{:S(2)}) collective-permute-start(f32[64,8]{0,1:T(8,128)S(1)} %get-tuple-element.66), channel_id=1, source_target_pairs={{0,2},{2,0},{1,3},{3,1},{4,6},{6,4},{5,7},{7,5},{8,10},{10,8},{9,1... | collective-permute-start | bytes 6152 | tf_op jit(solution)/shard_map/ppermute | solution.py:20
  43.2 3.6 %collective-permute-start.13 = (f32[64,8]{0,1:T(8,128)S(1)}, f32[64,8]{0,1:T(8,128)S(1)}, u32[]{:S(2)}, u32[]{:S(2)}) collective-permute-start(f32[64,8]{0,1:T(8,128)S(1)} %get-tuple-element.65), channel_id=1, source_target_pairs={{0,2},{2,0},{1,3},{3,1},{4,6},{6,4},{5,7},{7,5},{8,10},{10,8},{9,1... | collective-permute-start | bytes 6152 | tf_op jit(solution)/shard_map/ppermute | solution.py:20
  44.5 6.9 %collective-permute-start.19 = (f32[64,32]{0,1:T(8,128)S(1)}, f32[64,32]{0,1:T(8,128)S(1)}, u32[]{:S(2)}, u32[]{:S(2)}) collective-permute-start(f32[64,32]{0,1:T(8,128)S(1)} %get-tuple-element.58), channel_id=1, source_target_pairs={{0,2},{2,0},{1,3},{3,1},{4,6},{6,4},{5,7},{7,5},{8,10},{10,8},{9,1... | collective-permute-start | bytes 24584 | tf_op jit(solution)/shard_map/ppermute | solution.py:20
  45.2 6.2 %collective-permute-start.18 = (f32[64,32]{0,1:T(8,128)S(1)}, f32[64,32]{0,1:T(8,128)S(1)}, u32[]{:S(2)}, u32[]{:S(2)}) collective-permute-start(f32[64,32]{0,1:T(8,128)S(1)} %get-tuple-element.59), channel_id=1, source_target_pairs={{0,2},{2,0},{1,3},{3,1},{4,6},{6,4},{5,7},{7,5},{8,10},{10,8},{9,1... | collective-permute-start | bytes 24584 | tf_op jit(solution)/shard_map/ppermute | solution.py:20
  47.4 5.3 %collective-permute-start.14 = (f32[64,32]{0,1:T(8,128)S(1)}, f32[64,32]{0,1:T(8,128)S(1)}, u32[]{:S(2)}, u32[]{:S(2)}) collective-permute-start(f32[64,32]{0,1:T(8,128)S(1)} %get-tuple-element.56), channel_id=1, source_target_pairs={{0,12},{4,0},{8,4},{12,8},{1,13},{5,1},{9,5},{13,9},{2,14},{6,2},{... | collective-permute-start | bytes 24584 | tf_op jit(solution)/shard_map/ppermute | solution.py:20
  51.3 5.5 %collective-permute-start.17 = (f32[64,32]{0,1:T(8,128)S(1)}, f32[64,32]{0,1:T(8,128)S(1)}, u32[]{:S(2)}, u32[]{:S(2)}) collective-permute-start(f32[64,32]{0,1:T(8,128)S(1)} %get-tuple-element.55), channel_id=1, source_target_pairs={{0,4},{4,8},{8,12},{12,0},{1,5},{5,9},{9,13},{13,1},{2,6},{6,10},{... | collective-permute-start | bytes 24584 | tf_op jit(solution)/shard_map/ppermute | solution.py:20
  61.5 0.6 copy-start.3
  62.1 11.2 %collective-permute-start.27 = (f32[6,32]{1,0:T(8,128)S(1)}, f32[6,32]{1,0:T(8,128)S(1)}, u32[]{:S(2)}, u32[]{:S(2)}) collective-permute-start(f32[6,32]{1,0:T(8,128)S(1)} %bitcast.227), channel_id=1, source_target_pairs={{0,2},{2,0},{1,3},{3,1},{4,6},{6,4},{5,7},{7,5},{8,10},{10,8},{9,1... | collective-permute-start | bytes 2312 | tf_op jit(solution)/shard_map/ppermute | solution.py:20
  63.5 0.7 slice-start.1
  63.5 9.8 %collective-permute-start.26 = (f32[6,32]{1,0:T(8,128)S(1)}, f32[6,32]{1,0:T(8,128)S(1)}, u32[]{:S(2)}, u32[]{:S(2)}) collective-permute-start(f32[6,32]{1,0:T(8,128)S(1)} %bitcast.228), channel_id=1, source_target_pairs={{0,2},{2,0},{1,3},{3,1},{4,6},{6,4},{5,7},{7,5},{8,10},{10,8},{9,1... | collective-permute-start | bytes 2312 | tf_op jit(solution)/shard_map/ppermute | solution.py:20
  64.3 3.7 %collective-permute-start.20 = (f32[6,8]{1,0:T(8,128)S(1)}, f32[6,8]{1,0:T(8,128)S(1)}, u32[]{:S(2)}, u32[]{:S(2)}) collective-permute-start(f32[6,8]{1,0:T(8,128)S(1)} %bitcast.234), channel_id=1, source_target_pairs={{0,2},{2,0},{1,3},{3,1},{4,6},{6,4},{5,7},{7,5},{8,10},{10,8},{9,1... | collective-permute-start | bytes 584 | tf_op jit(solution)/shard_map/ppermute | solution.py:20
  65.7 3.6 %collective-permute-start.21 = (f32[6,8]{1,0:T(8,128)S(1)}, f32[6,8]{1,0:T(8,128)S(1)}, u32[]{:S(2)}, u32[]{:S(2)}) collective-permute-start(f32[6,8]{1,0:T(8,128)S(1)} %bitcast.233), channel_id=1, source_target_pairs={{0,2},{2,0},{1,3},{3,1},{4,6},{6,4},{5,7},{7,5},{8,10},{10,8},{9,1... | collective-permute-start | bytes 584 | tf_op jit(solution)/shard_map/ppermute | solution.py:20
  66.4 3.9 %collective-permute-start.23 = (f32[6,8]{1,0:T(8,128)S(1)}, f32[6,8]{1,0:T(8,128)S(1)}, u32[]{:S(2)}, u32[]{:S(2)}) collective-permute-start(f32[6,8]{1,0:T(8,128)S(1)} %bitcast.231), channel_id=1, source_target_pairs={{0,2},{2,0},{1,3},{3,1},{4,6},{6,4},{5,7},{7,5},{8,10},{10,8},{9,1... | collective-permute-start | bytes 584 | tf_op jit(solution)/shard_map/ppermute | solution.py:20
  68.0 3.6 %collective-permute-start.24 = (f32[6,8]{1,0:T(8,128)S(1)}, f32[6,8]{1,0:T(8,128)S(1)}, u32[]{:S(2)}, u32[]{:S(2)}) collective-permute-start(f32[6,8]{1,0:T(8,128)S(1)} %bitcast.232), channel_id=1, source_target_pairs={{0,2},{2,0},{1,3},{3,1},{4,6},{6,4},{5,7},{7,5},{8,10},{10,8},{9,1... | collective-permute-start | bytes 584 | tf_op jit(solution)/shard_map/ppermute | solution.py:20
  70.2 3.7 %collective-permute-start.22 = (f32[6,32]{1,0:T(8,128)S(1)}, f32[6,32]{1,0:T(8,128)S(1)}, u32[]{:S(2)}, u32[]{:S(2)}) collective-permute-start(f32[6,32]{1,0:T(8,128)S(1)} %scatter-add.37), channel_id=1, source_target_pairs={{0,12},{4,0},{8,4},{12,8},{1,13},{5,1},{9,5},{13,9},{2,14},{6,2},{... | collective-permute-start | bytes 2312 | tf_op jit(solution)/shard_map/ppermute | solution.py:20
  72.4 5.5 %collective-permute-start.25 = (f32[6,32]{1,0:T(8,128)S(1)}, f32[6,32]{1,0:T(8,128)S(1)}, u32[]{:S(2)}, u32[]{:S(2)}) collective-permute-start(f32[6,32]{1,0:T(8,128)S(1)} %scatter-add.38), channel_id=1, source_target_pairs={{0,4},{4,8},{8,12},{12,0},{1,5},{5,9},{9,13},{13,1},{2,6},{6,10},{... | collective-permute-start | bytes 2312 | tf_op jit(solution)/shard_map/ppermute | solution.py:20
where the time goes:
time: 80.8 us; the launch traced here: 80.4 us
  starting transfers between devices  34.9 us (43%)
  waiting for transfers between devices  19.5 us (24%)
  matrix products  9.9 us (12%)
  local copies, waits for them, and re-layouts  9.42 us (12%)
  other arithmetic  6.19 us (8%)
    ppermute x20, starting transfers between devices, passed_along(): lax.ppermute(value, axis, [(i, (i + by) % peers) for i in range(peers)])  21.7 us
    ppermute x20, waiting for transfers between devices, passed_along(): lax.ppermute(value, axis, [(i, (i + by) % peers) for i in range(peers)])  14.7 us
    ppermute x4, starting transfers between devices, padded(): lax.ppermute(tail, axis, [(i, (i + 1) % count) for i in range(count)])  7.14 us
    ppermute x4, starting transfers between devices, padded(): lax.ppermute(head, axis, [((i + 1) % count, i) for i in range(count)])  6.09 us
    unnamed x39, local copies, waits for them, and re-layouts  5.06 us
    dot_general x11, matrix products, project(): return jnp.einsum('mcd,mce->mde', weight, values, precision=highest)  4.24 us
    ppermute x4, waiting for transfers between devices, padded(): lax.ppermute(tail, axis, [(i, (i + 1) % count) for i in range(count)])  3.28 us
    dot_general x3, matrix products, advance(): jnp.einsum('mcs,se->mce', feature_table, join_hot, precision=highest)  2.78 us
  transfers between devices with their start and end apart: 28, of which 16 were waited for; matrix products, arithmetic and copies ran while one was open for 6% of the time, Pallas kernels for 0%

commit v1 on v0

v1 whole, which is shorter than its diff:
```python
import jax
import jax.numpy as jnp
from jax import lax
from jax.experimental import pallas as pl
from jax.experimental.pallas import tpu as pltpu
from jax.sharding import PartitionSpec as P

NEIGH = 16
box_edge = 20.0
energy_scale = 16.0
REACH = 3
LANES = 128
CHUNK = 8
PACK_ROWS = 24
f32 = jnp.float32
bf16 = jnp.bfloat16
i32 = jnp.int32


def iota(shape, dim):
    return lax.broadcasted_iota(i32, shape, dim)


def halves(x):
    hi = x.astype(bf16).astype(f32)
    return hi, x - hi


def pack_kernel(pos, species, centers, neighbours, masks, skin, out):
    tiles = centers.shape[-1] // LANES
    atoms = pos.shape[-1]
    ghosts = skin.shape[-1]
    out[...] = jnp.zeros(out.shape, f32)
    live = jnp.zeros((1, LANES), f32)
    for t in range(tiles):
        cut = slice(t * LANES, (t + 1) * LANES)
        out[t : t + 1, :] = centers[0, :, cut].astype(f32)
        out[tiles + t : tiles + t + 1, :] = neighbours[0, :, cut].astype(f32)
        live = live + masks[0, :, cut].astype(f32)
    base = 2 * tiles
    for q in range(3):
        row = pos[q, 0]
        out[base + q : base + q + 1, :] = jnp.concatenate([row, row], axis=1)
    row = species[0].astype(f32)
    out[base + 3 : base + 4, :] = jnp.concatenate([row, row], axis=1)
    out[base + 4 : base + 5, 0:ghosts] = skin[0].astype(f32)
    out[base + 5 : base + 6, :] = live


def block_diag(blocks):
    rows = []
    for at, block in enumerate(blocks):
        parts = [block if k == at else jnp.zeros((block.shape[0], other.shape[1]), f32) for k, other in enumerate(blocks)]
        rows.append(jnp.concatenate(parts, axis=1))
    return jnp.concatenate(rows, axis=0)


def split_left(matrix):
    hi, lo = halves(matrix)
    return jnp.concatenate(
        [jnp.concatenate([hi, hi], axis=1), jnp.concatenate([lo, jnp.zeros_like(lo)], axis=1)], axis=0
    ).astype(bf16)


def weights_kernel(embed, radial, w_mix, w_latent, w_update, readout, geo, dense, radial_back, columns):
    members, elements, channels = embed.shape
    width = members * channels
    embed_t = jnp.concatenate([embed[m].T for m in range(members)], axis=0)
    embed_t = jnp.concatenate([embed_t, jnp.zeros((width, 8 - elements), f32)], axis=1)
    radial_t = jnp.concatenate([radial[m].T for m in range(members)], axis=0)
    r_hi, r_lo = halves(radial_t)
    e_hi, e_lo = halves(embed_t)
    none = jnp.zeros_like(r_hi)
    geo[...] = jnp.concatenate(
        [
            jnp.concatenate([r_hi, r_hi, r_lo, none, none, none], axis=1),
            jnp.concatenate([none, none, none, e_hi, e_lo, none], axis=1),
        ],
        axis=0,
    ).astype(bf16)
    mix0 = block_diag([w_mix[m, 0] for m in range(members)])
    mix1 = block_diag([w_mix[m, 1] for m in range(members)])
    latent = block_diag([w_latent[m, 0] for m in range(members)])
    update0 = block_diag([w_update[m, 0] for m in range(members)])
    update1 = block_diag([w_update[m, 1] for m in range(members)])
    for at, matrix in enumerate((mix0.T, latent.T, mix1.T, mix1, latent, mix0, update0.T * (1.0 / NEIGH), update0 * (1.0 / NEIGH))):
        dense[at] = split_left(matrix)
    radial_back[...] = split_left(block_diag([radial[m] for m in range(members)]))
    read_row = jnp.concatenate([readout[m : m + 1, :] for m in range(members)], axis=1)
    eye = (iota((width, width), 0) == iota((width, width), 1)).astype(f32)
    read = jnp.sum(eye * read_row, axis=1, keepdims=True)
    pull = jnp.sum(update1 * read_row, axis=1, keepdims=True)
    columns[0] = jnp.broadcast_to(read * energy_scale, (width, LANES))
    columns[1] = jnp.broadcast_to(pull * (energy_scale / NEIGH), (width, LANES))


def lane_pick(table, lanes):
    return jnp.take_along_axis(table, jnp.broadcast_to(lanes, table.shape), axis=1, mode="promise_in_bounds")


def product(left, x):
    rows = left.shape[0] // 2
    hi, lo = halves(x)
    both = jnp.dot(left, jnp.concatenate([hi, lo], axis=0).astype(bf16), preferred_element_type=f32)
    return both[:rows] + both[rows:]


def sum_to(values, hot):
    hi, lo = halves(values)
    both = lax.dot_general(
        jnp.concatenate([hi, lo], axis=0).astype(bf16), hot, (((1,), (1,)), ((), ())), preferred_element_type=f32
    )
    return both[: values.shape[0]] + both[values.shape[0] :]


def silu_and_slope(x):
    s = 0.5 * jnp.tanh(0.5 * x) + 0.5
    value = x * s
    return value, s + value * (1.0 - s)


def sin_cos(x):
    turns = jnp.floor(x * 0.15915494309189535 + 0.5)
    r = (x - turns * 6.28125) - turns * 1.9353071795864769e-3
    h = 0.5 * r
    q = h * h
    s = h * (1.0 + q * (-1 / 6 + q * (1 / 120 + q * (-1 / 5040 + q * (1 / 362880 + q * (-1 / 39916800 + q * (1 / 6227020800)))))))
    c = 1.0 + q * (-1 / 2 + q * (1 / 24 + q * (-1 / 720 + q * (1 / 40320 + q * (-1 / 3628800 + q * (1 / 479001600 - q * (1 / 87178291200)))))))
    return 2.0 * s * c, 1.0 - 2.0 * s * s


def force_kernel(wx, wy, place, n_in, *refs):
    arrived = refs[:n_in]
    geo, dense, radial_back, columns, out = refs[n_in : n_in + 5]
    (raw, posb, lid_s, cl_s, spc, spn, unit, basis_s, slope_s, feats, sums, grads, pulls,
     joined_s, lat_s, dpre_s, dz_s, back_s, total, tile_list, near_list) = refs[n_in + 5 :]
    tiles = 8
    n_dom = wx * wy
    nv = (wy + 1) // 2
    n_src = 3 * nv
    n_blk = wx * nv
    width = feats.shape[1]
    members = out.shape[0]
    own_a, own_b, slots = place()

    for ref, at, slot in slots:
        raw[slot] = arrived[ref][at * PACK_ROWS : (at + 1) * PACK_ROWS, :]

    none = n_dom * tiles
    count = jnp.int32(0)
    near = jnp.int32(0)
    for d in range(n_dom):
        a, b = d // wy, d % wy
        live = jnp.max(raw[d, 2 * tiles + 5 : 2 * tiles + 6, :]).astype(i32)
        da = lax.rem(a - own_a + 1 + wx, wx)
        db = lax.rem(b - own_b + 1 + wy, wy)
        touches = jnp.logical_and(da < 3, db < 3)
        for t in range(tiles):
            tile_list[count + t] = d * tiles + t
            near_list[near + t] = d * tiles + t
        count = count + live
        near = near + jnp.where(touches, live, 0)
    for t in range(CHUNK):
        tile_list[count + t] = none
        near_list[near + t] = none

    lane = iota((8, LANES), 1)
    for a in range(wx):
        for v in range(nv):
            low = raw[a * wy + 2 * v, 2 * tiles : 2 * tiles + 8, :]
            high = raw[a * wy + min(2 * v + 1, wy - 1), 2 * tiles : 2 * tiles + 8, :]
            posb[a * nv + v] = jnp.where(lane < 64, low, high)

    lid_s[none : none + 8, :] = jnp.full((8, LANES), -1, i32)
    cl_s[none : none + 8, :] = jnp.full((8, LANES), -1, i32)
    for ref in (spc, spn):
        ref[none : none + 8, :] = jnp.zeros((8, LANES), i32)
    unit[:, none : none + 8, :] = jnp.zeros((3, 8, LANES), f32)
    basis_s[none * 8 : none * 8 + 8, :] = jnp.zeros((8, LANES), f32)
    slope_s[none * 8 : none * 8 + 8, :] = jnp.zeros((8, LANES), f32)

    row = lane[0:1]
    for d in range(n_dom):
        a, b = d // wy, d % wy

        def ids(u, v, start):
            src = ((a + u - 1) % wx) * wy + (b + v - 1) % wy
            base = u * nv * LANES + ((b + v - 1) % wy) * 64 + 8192 * v
            skin = raw[src, 2 * tiles + 4 : 2 * tiles + 5, :].astype(i32) + base
            return pltpu.roll(skin, start, 1) if start else skin

        first = row + (nv * LANES + b * 64 + 8192)
        first = jnp.where(row >= 64, ids(0, 1, 64), first)
        first = jnp.where(row >= 96, ids(1, 0, 96), first)
        second = ids(1, 2, 0)
        second = jnp.where(row >= 32, ids(2, 1, 32), second)
        for k, (u, v) in enumerate(((0, 0), (0, 2), (2, 0), (2, 2))):
            second = jnp.where(row >= 64 + 8 * k, ids(u, v, 64 + 8 * k), second)
        center = raw[d, 0:tiles, :].astype(i32)
        entry = raw[d, tiles : 2 * tiles, :].astype(i32)
        wide = (8, LANES)
        code = jnp.where(
            entry < LANES,
            lane_pick(jnp.broadcast_to(first, wide), entry & 127),
            lane_pick(jnp.broadcast_to(second, wide), entry & 127),
        )
        side_y = lax.shift_right_logical(code, 13)
        lid = code & 8191
        side_x = (lid >= nv * LANES).astype(f32) + (lid >= 2 * nv * LANES).astype(f32) - 1.0
        clid = center + b * 64
        block = lax.shift_right_logical(lid, 7)
        got_n, got_c = [], []
        for q in range(4):
            value = None
            for s in range(n_src):
                src = ((a + s // nv - 1) % wx) * nv + s % nv
                picked = lane_pick(jnp.broadcast_to(posb[src, q : q + 1, :], wide), lid & 127)
                value = picked if value is None else jnp.where(block == s, picked, value)
            got_n.append(value)
            got_c.append(lane_pick(jnp.broadcast_to(posb[a * nv + b // 2, q : q + 1, :], wide), clid & 127))
        dx = got_n[0] + box_edge * side_x - got_c[0]
        dy = got_n[1] + box_edge * (side_y.astype(f32) - 1.0) - got_c[1]
        dz = got_n[2] - got_c[2]
        distance = jnp.sqrt(dx * dx + dy * dy + dz * dz + 1.0)
        inverse = 1.0 / distance
        cut = slice(d * tiles, (d + 1) * tiles)
        for q, part in enumerate((dx, dy, dz)):
            unit[q, cut, :] = part * inverse
        spn[cut, :] = got_n[3].astype(i32)
        spc[cut, :] = got_c[3].astype(i32)
        lid_s[cut, :] = lid
        cl_s[cut, :] = clid
        s1, c1 = sin_cos(distance * 0.25)
        env = jnp.exp(distance * (-1.0 / 32.0))
        c_k, s_k = [jnp.ones_like(c1), c1], [jnp.zeros_like(s1), s1]
        for k in range(2, 8):
            c_k.append(2.0 * c1 * c_k[-1] - c_k[-2])
            s_k.append(2.0 * c1 * s_k[-1] - s_k[-2])
        for k in range(8):
            basis = c_k[k] * env
            basis_s[pl.ds(d * 64 + k, 8, stride=8), :] = basis
            slope_s[pl.ds(d * 64 + k, 8, stride=8), :] = s_k[k] * env * (-k / 4.0) - basis * (1.0 / 32.0)

    for ref in (sums, grads):
        ref[...] = jnp.zeros(ref.shape, f32)
    for ref in (joined_s, lat_s, dpre_s, dz_s, back_s):
        ref[none] = jnp.zeros((width, LANES), f32)
    total[...] = jnp.zeros(total.shape, f32)

    def spots(tau):
        d = lax.shift_right_logical(tau, 3)
        a, b = lax.div(d, wy), lax.rem(d, wy)
        sources = [lax.rem(a + (s // nv - 1 + wx), wx) * nv + s % nv for s in range(n_src)]
        home = lax.rem(a, wx) * nv + lax.div(b, 2)
        return sources, home, lax.div(b, 2)

    atom = iota((LANES, LANES), 0)

    def hot(ids_row):
        return jnp.where(atom == ids_row, 1.0, 0.0)

    def side(parts):
        return jnp.concatenate(parts, axis=1)

    def forward(chunk, carry):
        taus = [tile_list[chunk * CHUNK + j] for j in range(CHUNK)]
        rhs = []
        sub = iota((8, LANES), 0)
        for tau in taus:
            hi, lo = halves(basis_s[pl.ds(pl.multiple_of(tau * 8, 8), 8), :])
            kinds = (sub == spc[pl.ds(tau, 1), :]).astype(f32) + (sub == spn[pl.ds(tau, 1), :]).astype(f32)
            rhs.append(jnp.concatenate([hi, lo, hi, kinds, kinds, jnp.zeros_like(hi)], axis=0).astype(bf16))
        both = jnp.dot(geo[...], side(rhs), preferred_element_type=f32)
        latent, latent_slope = silu_and_slope(both[:width])
        joined = both[width:]
        active, slope = silu_and_slope(product(dense[0], latent * joined))
        latent = latent + product(dense[1], active)
        for j, tau in enumerate(taus):
            cut = slice(j * LANES, (j + 1) * LANES)
            joined_s[tau] = joined[:, cut]
            dpre_s[tau] = latent_slope[:, cut]
            dz_s[tau] = slope[:, cut]
            lat_s[tau] = latent[:, cut]
            _, home, half = spots(tau)
            ids_row = cl_s[pl.ds(tau, 1), :] - half * LANES
            sums[home] += sum_to(active[:, cut], hot(ids_row).astype(bf16))
        return carry

    chunks = lax.div(count + (CHUNK - 1), CHUNK)
    lax.fori_loop(0, chunks, forward, 0)

    sub = iota((8, LANES), 0)
    for k in range(n_blk):
        kinds = (sub == posb[k, 3:4, :].astype(i32)).astype(f32)
        empty = jnp.zeros_like(kinds)
        rhs = jnp.concatenate([empty, empty, empty, kinds, kinds, empty], axis=0).astype(bf16)
        start = jnp.dot(geo[...], rhs, preferred_element_type=f32)[width:]
        feats[k] = start + product(dense[6], sums[k])

    def middle(chunk, carry):
        taus = [tile_list[chunk * CHUNK + j] for j in range(CHUNK)]
        joined, lids, places = [], [], []
        for tau in taus:
            sources, home, half = spots(tau)
            lid = lid_s[pl.ds(tau, 1), :]
            clid = cl_s[pl.ds(tau, 1), :]
            block = jnp.broadcast_to(lax.shift_right_arithmetic(lid, 7), (width, LANES))
            value = None
            for s in range(n_src):
                picked = lane_pick(feats[sources[s]], lid & 127)
                value = picked if value is None else jnp.where(block == s, picked, value)
            joined.append(value + lane_pick(feats[home], clid & 127))
            lids.append((lid, clid - half * LANES))
            places.append((sources, home, half))
        joined = side(joined)
        latent = side([lat_s[tau] for tau in taus])
        _, slope = silu_and_slope(product(dense[2], latent * joined))
        dmix = product(dense[3], side([columns[1]] * CHUNK) * slope)
        back = dmix * joined
        spread = dmix * latent
        for j, tau in enumerate(taus):
            cut = slice(j * LANES, (j + 1) * LANES)
            back_s[tau] = back[:, cut]
            sources, home, half = places[j]
            lid, clid = lids[j]
            hots = [hot(lid - s * LANES) for s in range(n_src)]
            own = hot(clid)
            for v in range(nv):
                here = own if nv == 1 else jnp.where(half == v, own, 0.0)
                hots[nv + v] = hots[nv + v] + here
            added = sum_to(spread[:, cut], jnp.concatenate(hots, axis=0).astype(bf16))
            for s in range(n_src):
                grads[sources[s]] += added[:, s * LANES : (s + 1) * LANES]
        return carry

    lax.fori_loop(0, chunks, middle, 0)

    for k in range(n_blk):
        pulls[k] = product(dense[7], grads[k] + columns[0])

    own_block = own_a * nv + lax.div(own_b, 2)

    def backward(chunk, carry):
        taus = [near_list[chunk * CHUNK + j] for j in range(CHUNK)]
        pulled = []
        for tau in taus:
            _, home, _ = spots(tau)
            pulled.append(lane_pick(pulls[home], cl_s[pl.ds(tau, 1), :] & 127))
        back = side([back_s[tau] for tau in taus])
        active = side(pulled) + product(dense[4], back)
        dmix = product(dense[5], active * side([dz_s[tau] for tau in taus]))
        dlat = back + dmix * side([joined_s[tau] for tau in taus])
        dbasis = product(radial_back[...], dlat * side([dpre_s[tau] for tau in taus]))
        moved = total[...]
        for j, tau in enumerate(taus):
            cut = slice(j * LANES, (j + 1) * LANES)
            slope = slope_s[pl.ds(pl.multiple_of(tau * 8, 8), 8), :]
            rows = []
            for m in range(members):
                along = jnp.sum(dbasis[m * 8 : (m + 1) * 8, cut] * slope, axis=0, keepdims=True)
                rows += [along * unit[q, pl.ds(tau, 1), :] for q in range(3)]
            rows.append(jnp.zeros((8 - 3 * members, LANES), f32))
            sources, home, half = spots(tau)
            lid = lid_s[pl.ds(tau, 1), :]
            clid = cl_s[pl.ds(tau, 1), :]
            hit = jnp.full((1, LANES), -1, i32)
            for s in range(n_src):
                this = jnp.where(sources[s] == own_block, s, -2)
                hit = jnp.where(lax.shift_right_arithmetic(lid, 7) == this, lid & 127, hit)
            chit = jnp.where(home == own_block, clid - half * LANES, -1)
            many = hot(hit) - hot(chit)
            moved = moved + sum_to(jnp.concatenate(rows, axis=0), many.astype(bf16))
        total[...] = moved
        return carry

    lax.fori_loop(0, lax.div(near + (CHUNK - 1), CHUNK), backward, 0)

    result = -total[...]
    result = jnp.where(lax.rem(own_b, 2) == 1, pltpu.roll(result, 64, 1), result)
    for m in range(members):
        for q in range(3):
            out[m, q, 0] = result[m * 3 + q : m * 3 + q + 1, 0:64]


def window(size):
    return min(size, 2 * REACH + 1)


def shift(value, axis, by):
    peers = lax.axis_size(axis)
    return lax.ppermute(value, axis, [(i, (i + by) % peers) for i in range(peers)])


def swap(value, dx, dy):
    nx, ny = lax.axis_size("gx"), lax.axis_size("gy")
    pairs = [(a * ny + b, (a ^ dx) * ny + (b ^ dy)) for a in range(nx) for b in range(ny)]
    return lax.ppermute(value, ("gx", "gy"), pairs)


def gathered(own, gx, gy):
    if gx == 4 and gy == 2:
        pair = jnp.concatenate([own, swap(own, 2, 0)], axis=0)
        arrays = [pair, swap(pair, 1, 0), swap(pair, 0, 1), swap(pair, 1, 1)]

        def place():
            a, b = lax.axis_index("gx"), lax.axis_index("gy")
            slots = []
            for k in range(4):
                for at in range(2):
                    slots.append((k, at, (a ^ ((k & 1) | (2 * at))) * 2 + (b ^ (k >> 1))))
            return a, b, slots

        return arrays, place
    wx, wy = window(gx), window(gy)
    steps = list(range(wy // 2 + 1)) + list(range(wy // 2 + 1 - wy, 0))
    column = jnp.concatenate([own if s == 0 else shift(own, "gy", -s) for s in steps], axis=0)
    steps_x = list(range(wx // 2 + 1)) + list(range(wx // 2 + 1 - wx, 0))
    arrays = [column if s == 0 else shift(column, "gx", -s) for s in steps_x]

    def place():
        slots = [(k, at, k * wy + at) for k in range(wx) for at in range(wy)]
        return jnp.int32(0), jnp.int32(0), slots

    return arrays, place


def on_device(
    positions, species, centers, neighbours, masks, skin, embed, radial, w_mix, w_latent, w_update, readout
):
    gx, gy = lax.axis_size("gx"), lax.axis_size("gy")
    atoms = positions.shape[-1]
    members, _, channels = embed.shape
    width = members * channels
    own = pl.pallas_call(
        pack_kernel, out_shape=jax.ShapeDtypeStruct((PACK_ROWS, LANES), f32), name="pack"
    )(positions, species, centers, neighbours, masks, skin)
    parts = pl.pallas_call(
        weights_kernel,
        out_shape=(
            jax.ShapeDtypeStruct((2 * width, 48), bf16),
            jax.ShapeDtypeStruct((8, 2 * width, 2 * width), bf16),
            jax.ShapeDtypeStruct((2 * members * 8, 2 * width), bf16),
            jax.ShapeDtypeStruct((2, width, LANES), f32),
        ),
        name="weights",
    )(embed, radial, w_mix, w_latent, w_update, readout)
    arrays, place = gathered(own, gx, gy)
    wx, wy = window(gx), window(gy)
    n_dom = wx * wy
    n_tiles = n_dom * 8
    n_blk = wx * ((wy + 1) // 2)
    per_tile = pltpu.VMEM((n_tiles + 1, width, LANES), f32)
    per_block = pltpu.VMEM((n_blk, width, LANES), f32)
    row_ids = pltpu.VMEM((n_tiles + 8, LANES), i32)

    def body(*refs):
        force_kernel(wx, wy, place, len(arrays), *refs)

    return pl.pallas_call(
        body,
        out_shape=jax.ShapeDtypeStruct((members, 3, 1, 1, atoms), f32),
        scratch_shapes=[
            pltpu.VMEM((n_dom, PACK_ROWS, LANES), f32),
            pltpu.VMEM((n_blk, 8, LANES), f32),
            row_ids,
            row_ids,
            row_ids,
            row_ids,
            pltpu.VMEM((3, n_tiles + 8, LANES), f32),
            pltpu.VMEM((n_tiles * 8 + 8, LANES), f32),
            pltpu.VMEM((n_tiles * 8 + 8, LANES), f32),
            per_block,
            per_block,
            per_block,
            per_block,
            per_tile,
            per_tile,
            per_tile,
            per_tile,
            per_tile,
            pltpu.VMEM((8, LANES), f32),
            pltpu.SMEM((n_tiles + 2 * CHUNK,), i32),
            pltpu.SMEM((n_tiles + 2 * CHUNK,), i32),
        ],
        compiler_params=pltpu.CompilerParams(vmem_limit_bytes=56 * 1024 * 1024),
        name="forces",
    )(*arrays, *parts)


def solution(mesh):
    return jax.shard_map(
        on_device,
        mesh=mesh,
        in_specs=(
            P(None, ("groups", "gx"), "gy", None),
            P(("groups", "gx"), "gy", None),
            P(("groups", "gx"), "gy", None),
            P(("groups", "gx"), "gy", None),
            P(("groups", "gx"), "gy", None),
            P(("groups", "gx"), "gy", None),
            P("gz", None, None),
            P("gz", None, None),
            P("gz", None, None, None),
            P("gz", None, None, None),
            P("gz", None, None, None),
            P("gz", None),
        ),
        out_specs=P("gz", None, ("groups", "gx"), "gy", None),
        check_vma=False,
    )
```

time: 80.8 us -> 35.4 us (0.44)
  starting transfers between devices: 34.9 us -> 7.52 us
  Pallas kernels: 0 us -> 22.8 us
  waiting for transfers between devices: 19.5 us -> 2.86 us
  matrix products: 9.9 us -> 0 us
  local copies, waits for them, and re-layouts: 9.42 us -> 1.21 us
  other arithmetic: 6.19 us -> 0.71 us
    ppermute x28 -> x4, starting transfers between devices: 34.9 us -> 7.52 us  [swap(): return lax.ppermute(value, ('gx', 'gy'), pairs)]
    pallas_call x0 -> x3, Pallas kernels: none -> 22.8 us  [the longest x1 19.3 us: on_device(): pl.pallas_call(body, out_shape=jax.ShapeDtypeStruct((members, 3, 1, 1, at...]
    ppermute x28 -> x4, waiting for transfers between devices: 19.5 us -> 2.86 us  [swap(): return lax.ppermute(value, ('gx', 'gy'), pairs)]
    dot_general x20 -> x0, matrix products: 9.9 us -> none  [the longest x11 4.24 us: project(): return jnp.einsum('mcd,mce->mde', weight, values, precision=highest)]
    scatter-add x3 -> x0, other arithmetic: 3.93 us -> none  [the longest x1 1.64 us: on_device(): feature_grad = table_grad[:, :, :atom_count].at[:, :, send_list].add(back...]
    unnamed x39 -> x11, local copies, waits for them, and re-layouts: 5.06 us -> 1.21 us
    another operation x3 -> x0, other arithmetic: 1.94 us -> none
    reshape x10 -> x0, local copies, waits for them, and re-layouts: 1.25 us -> none  [the longest x1 0.67 us: on_device(): return (-own_grad).reshape(member_count, 3, 1, 1, atom_count)]
  transfers between devices with their start and end apart: 28 -> 4, of which waited for: 16 -> 3; matrix products, arithmetic and copies ran while one was open for 6% -> 2% of each run, Pallas kernels for 0% -> 6%
where the time goes in v1:
time: 35.4 us; the launch traced here: 35.1 us
  Pallas kernels  22.8 us (64%)
  starting transfers between devices  7.52 us (21%)
  waiting for transfers between devices  2.86 us (8%)
  local copies, waits for them, and re-layouts  1.21 us (3%)
  other arithmetic  0.71 us (2%)
    pallas_call x1, Pallas kernels, on_device(): pl.pallas_call(body, out_shape=jax.ShapeDtypeStruct((members, 3, 1, 1, at...  19.3 us
    ppermute x4, starting transfers between devices, swap(): return lax.ppermute(value, ('gx', 'gy'), pairs)  7.52 us
    ppermute x4, waiting for transfers between devices, swap(): return lax.ppermute(value, ('gx', 'gy'), pairs)  2.86 us
    pallas_call x1, Pallas kernels, on_device(): pl.pallas_call(weights_kernel, out_shape=(jax.ShapeDtypeStruct((2 * width...  2.11 us
    pallas_call x1, Pallas kernels, on_device(): pl.pallas_call(pack_kernel, out_shape=jax.ShapeDtypeStruct((PACK_ROWS, LA...  1.42 us
    unnamed x11, local copies, waits for them, and re-layouts  1.21 us
    concatenate x1, other arithmetic, gathered(): pair = jnp.concatenate([own, swap(own, 2, 0)], axis=0)  0.71 us
  transfers between devices with their start and end apart: 4, of which 3 were waited for; matrix products, arithmetic and copies ran while one was open for 2% of the time, Pallas kernels for 6%

profile of v1, /device:TPU:0, one launch (start us, length us, event | category | flops | bytes accessed | tf_op | source)
XLA Modules:
  0.0 35.1 jit_solution(2812091297462522861)
XLA Ops:
  0.0 1.4 %pack.1 = f32[24,128]{1,0:T(8,128)} custom-call(f32[3,1,1,64]{3,2,1,0:T(1,128)} %pos.1, s32[1,1,64]{2,1,0:T(1,128)} %species.1, s32[1,1,1024]{2,1,0:T(1,128)} %centers.1, s32[1,1,1024]{2,1,0:T(1,128)} %neighbours.1, s32[1,1,1024]{2,1,0:T(1,128)} %masks.1, s32[1,1,32]{2,1,0:T(1,128)} %skin.1), custom_call_target="tpu_custom_call" | custom-call | tf_op jit(solution)/shard_map/pack/pallas_call | solution.py:434
  1.4 0.0 copy-start.4
  1.4 4.0 %collective-permute-start = (f32[24,128]{1,0:T(8,128)}, f32[24,128]{1,0:T(8,128)S(1)}, u32[]{:S(2)}, u32[]{:S(2)}) collective-permute-start(f32[24,128]{1,0:T(8,128)} %pack.1), channel_id=1, source_target_pairs={{0,8},{2,10},{4,12},{6,14},{8,0},{10,2},{12,4},{14,6},{1,9},{3,11}... | collective-permute-start | bytes 36872 | tf_op jit(solution)/shard_map/ppermute | solution.py:397
  5.5 1.9 %collective-permute-done = f32[24,128]{1,0:T(8,128)S(1)} collective-permute-done((f32[24,128]{1,0:T(8,128)}, f32[24,128]{1,0:T(8,128)S(1)}, u32[]{:S(2)}, u32[]{:S(2)}) %collective-permute-start) | collective-permute-done | bytes 12320 | tf_op jit(solution)/shard_map/ppermute | solution.py:397
  7.3 0.7 %pad_maximum_fusion.refs_0_ = f32[48,128]{1,0:T(8,128)S(1)} fusion(f32[24,128]{1,0:T(8,128)S(1)} %collective-permute-done, f32[24,128]{1,0:T(8,128)} %pack.1), kind=kLoop, calls=%fused_computation | loop fusion | flops 6144 | bytes 49152 | tf_op jit(solution)/shard_map/concatenate | solution.py:402
  8.1 0.0 copy-start
  8.1 2.8 %collective-permute-start.3 = (f32[48,128]{1,0:T(8,128)S(1)}, f32[48,128]{1,0:T(8,128)S(1)}, u32[]{:S(2)}, u32[]{:S(2)}) collective-permute-start(f32[48,128]{1,0:T(8,128)S(1)} %pad_maximum_fusion.refs_0_), channel_id=1, source_target_pairs={{0,6},{2,4},{4,2},{6,0},{8,14},{10,12},{12,10},{14,8},{1,7},{3,5},... | collective-permute-start | bytes 73736 | tf_op jit(solution)/shard_map/ppermute | solution.py:397
  10.9 0.5 %collective-permute-start.2 = (f32[48,128]{1,0:T(8,128)S(1)}, f32[48,128]{1,0:T(8,128)S(1)}, u32[]{:S(2)}, u32[]{:S(2)}) collective-permute-start(f32[48,128]{1,0:T(8,128)S(1)} %pad_maximum_fusion.refs_0_), channel_id=1, source_target_pairs={{0,2},{2,0},{4,6},{6,4},{8,10},{10,8},{12,14},{14,12},{1,3},{3,1},... | collective-permute-start | bytes 73736 | tf_op jit(solution)/shard_map/ppermute | solution.py:397
  11.4 0.1 collective-permute-start.1
  11.5 0.0 copy-done.4
  11.5 0.6 %copy.13.embed = f32[2,5,32]{2,1,0:T(8,128)} copy(f32[2,5,32]{2,0,1:T(2,128)S(1)} %copy-done.4) | data formatting | bytes 2560 | tf_op args[6]
  12.1 2.1 %weights.1 = (bf16[128,48]{1,0:T(8,128)(2,1)}, bf16[8,128,128]{2,1,0:T(8,128)(2,1)}, bf16[32,128]{1,0:T(8,128)(2,1)}, f32[2,64,128]{2,1,0:T(8,128)}) custom-call(f32[2,5,32]{2,1,0:T(8,128)} %copy.13.embed, f32[2,8,32]{2,1,0:T(8,128)} %radial.1, f32[2,2,32,32]{3,2,1,0:T(8,128)} %w_mix.1, f32[2,1,32,32]{3,2,1,0:T(8,128)} %w_latent.1, ...), custom_call_target="tpu_custom_call" | custom-call | tf_op jit(solution)/shard_map/weights/pallas_call | solution.py:437
  14.3 0.0 copy-done
  14.3 0.0 collective-permute-done.3.refs_3_
  14.3 0.0 copy-start.1
  14.3 0.4 %collective-permute-done.2.refs_2_ = f32[48,128]{1,0:T(8,128)S(1)} collective-permute-done((f32[48,128]{1,0:T(8,128)S(1)}, f32[48,128]{1,0:T(8,128)S(1)}, u32[]{:S(2)}, u32[]{:S(2)}) %collective-permute-start.2) | collective-permute-done | bytes 24608 | tf_op jit(solution)/shard_map/ppermute | solution.py:397
  14.7 0.0 copy-start.2
  14.7 0.5 %collective-permute-done.1.refs_1_ = f32[48,128]{1,0:T(8,128)S(1)} collective-permute-done((f32[48,128]{1,0:T(8,128)S(1)}, f32[48,128]{1,0:T(8,128)S(1)}, u32[]{:S(2)}, u32[]{:S(2)}) %collective-permute-start.1) | collective-permute-done | bytes 24608 | tf_op jit(solution)/shard_map/ppermute | solution.py:397
  15.3 0.0 copy-start.3
  15.3 0.0 copy-done.1
  15.3 0.1 copy-done.2
  15.3 0.5 %copy-done.3 = f32[48,128]{1,0:T(8,128)} copy-done((f32[48,128]{1,0:T(8,128)}, f32[48,128]{1,0:T(8,128)S(1)}, u32[]{:S(2)}) %copy-start.3) | copy-done | bytes 24600
  15.9 19.3 %forces.1 = f32[2,3,1,1,64]{4,3,2,1,0:T(1,128)} custom-call(f32[48,128]{1,0:T(8,128)} %copy-done, f32[48,128]{1,0:T(8,128)} %copy-done.3, f32[48,128]{1,0:T(8,128)} %copy-done.2, f32[48,128]{1,0:T(8,128)} %copy-done.1, bf16[128,48]{1,0:T(8,128)(2,1)} %get-tuple-element.9.refs_4_, bf16[8,128,128]{2,1,0:T(8,128)(2,1)} %get-tuple-element.10.refs_5_, ...), custom_call_target="tpu_custom_call" | custom-call | tf_op jit(solution)/shard_map/forces/pallas_call | solution.py:459
Async XLA Ops:
  1.4 10.1 %copy-start.4 = (f32[2,5,32]{2,0,1:T(2,128)S(1)}, f32[2,5,32]{2,0,1:T(2,128)}, u32[]{:S(2)}) copy-start(f32[2,5,32]{2,0,1:T(2,128)} %param.18) | copy-start | bytes 3844
  1.4 5.9 %collective-permute-start = (f32[24,128]{1,0:T(8,128)}, f32[24,128]{1,0:T(8,128)S(1)}, u32[]{:S(2)}, u32[]{:S(2)}) collective-permute-start(f32[24,128]{1,0:T(8,128)} %pack.1), channel_id=1, source_target_pairs={{0,8},{2,10},{4,12},{6,14},{8,0},{10,2},{12,4},{14,6},{1,9},{3,11}... | collective-permute-start | bytes 36872 | tf_op jit(solution)/shard_map/ppermute | solution.py:397
  8.1 6.2 %copy-start = (f32[48,128]{1,0:T(8,128)}, f32[48,128]{1,0:T(8,128)S(1)}, u32[]{:S(2)}) copy-start(f32[48,128]{1,0:T(8,128)S(1)} %pad_maximum_fusion.refs_0_) | copy-start | bytes 73732
  8.1 6.2 %collective-permute-start.3 = (f32[48,128]{1,0:T(8,128)S(1)}, f32[48,128]{1,0:T(8,128)S(1)}, u32[]{:S(2)}, u32[]{:S(2)}) collective-permute-start(f32[48,128]{1,0:T(8,128)S(1)} %pad_maximum_fusion.refs_0_), channel_id=1, source_target_pairs={{0,6},{2,4},{4,2},{6,0},{8,14},{10,12},{12,10},{14,8},{1,7},{3,5},... | collective-permute-start | bytes 73736 | tf_op jit(solution)/shard_map/ppermute | solution.py:397
  10.9 3.8 %collective-permute-start.2 = (f32[48,128]{1,0:T(8,128)S(1)}, f32[48,128]{1,0:T(8,128)S(1)}, u32[]{:S(2)}, u32[]{:S(2)}) collective-permute-start(f32[48,128]{1,0:T(8,128)S(1)} %pad_maximum_fusion.refs_0_), channel_id=1, source_target_pairs={{0,2},{2,0},{4,6},{6,4},{8,10},{10,8},{12,14},{14,12},{1,3},{3,1},... | collective-permute-start | bytes 73736 | tf_op jit(solution)/shard_map/ppermute | solution.py:397
  11.4 3.8 %collective-permute-start.1 = (f32[48,128]{1,0:T(8,128)S(1)}, f32[48,128]{1,0:T(8,128)S(1)}, u32[]{:S(2)}, u32[]{:S(2)}) collective-permute-start(f32[48,128]{1,0:T(8,128)S(1)} %pad_maximum_fusion.refs_0_), channel_id=1, source_target_pairs={{0,4},{2,6},{4,0},{6,2},{8,12},{10,14},{12,8},{14,10},{1,5},{3,7},... | collective-permute-start | bytes 73736 | tf_op jit(solution)/shard_map/ppermute | solution.py:397
  14.3 1.0 %copy-start.1 = (f32[48,128]{1,0:T(8,128)}, f32[48,128]{1,0:T(8,128)S(1)}, u32[]{:S(2)}) copy-start(f32[48,128]{1,0:T(8,128)S(1)} %collective-permute-done.3.refs_3_) | copy-start | bytes 73732
  14.7 0.6 %copy-start.2 = (f32[48,128]{1,0:T(8,128)}, f32[48,128]{1,0:T(8,128)S(1)}, u32[]{:S(2)}) copy-start(f32[48,128]{1,0:T(8,128)S(1)} %collective-permute-done.2.refs_2_) | copy-start | bytes 73732
  15.3 0.6 %copy-start.3 = (f32[48,128]{1,0:T(8,128)}, f32[48,128]{1,0:T(8,128)S(1)}, u32[]{:S(2)}) copy-start(f32[48,128]{1,0:T(8,128)S(1)} %collective-permute-done.1.refs_1_) | copy-start | bytes 73732

commit v2 on v1

--- a/solution.py
+++ b/solution.py
@@ -57,9 +57,12 @@
 
 def split_left(matrix):
     hi, lo = halves(matrix)
-    return jnp.concatenate(
-        [jnp.concatenate([hi, hi], axis=1), jnp.concatenate([lo, jnp.zeros_like(lo)], axis=1)], axis=0
-    ).astype(bf16)
+    return jnp.concatenate([hi, hi, lo], axis=1).astype(bf16)
+
+
+def parts(x):
+    hi = x.astype(bf16)
+    return hi, (x - hi.astype(f32)).astype(bf16)
 
 
 def weights_kernel(embed, radial, w_mix, w_latent, w_update, readout, geo, dense, radial_back, columns):
@@ -68,7 +71,7 @@
     embed_t = jnp.concatenate([embed[m].T for m in range(members)], axis=0)
     embed_t = jnp.concatenate([embed_t, jnp.zeros((width, 8 - elements), f32)], axis=1)
     radial_t = jnp.concatenate([radial[m].T for m in range(members)], axis=0)
-    r_hi, r_lo = halves(radial_t)
+    r_hi, r_lo = halves(0.5 * radial_t)
     e_hi, e_lo = halves(embed_t)
     none = jnp.zeros_like(r_hi)
     geo[...] = jnp.concatenate(
@@ -83,15 +86,18 @@
     latent = block_diag([w_latent[m, 0] for m in range(members)])
     update0 = block_diag([w_update[m, 0] for m in range(members)])
     update1 = block_diag([w_update[m, 1] for m in range(members)])
-    for at, matrix in enumerate((mix0.T, latent.T, mix1.T, mix1, latent, mix0, update0.T * (1.0 / NEIGH), update0 * (1.0 / NEIGH))):
-        dense[at] = split_left(matrix)
-    radial_back[...] = split_left(block_diag([radial[m] for m in range(members)]))
+    radial_back[...] = split_left(0.5 * block_diag([radial[m] for m in range(members)]))
     read_row = jnp.concatenate([readout[m : m + 1, :] for m in range(members)], axis=1)
     eye = (iota((width, width), 0) == iota((width, width), 1)).astype(f32)
     read = jnp.sum(eye * read_row, axis=1, keepdims=True)
-    pull = jnp.sum(update1 * read_row, axis=1, keepdims=True)
-    columns[0] = jnp.broadcast_to(read * energy_scale, (width, LANES))
-    columns[1] = jnp.broadcast_to(pull * (energy_scale / NEIGH), (width, LANES))
+    pull = jnp.sum(update1.T * read, axis=0, keepdims=True) * (energy_scale / NEIGH)
+    columns[...] = jnp.broadcast_to(read * energy_scale, (width, LANES))
+    factors = (
+        0.5 * mix0.T, latent.T, 0.5 * mix1.T, 0.5 * mix1 * pull, latent, 0.5 * mix0,
+        update0.T * (1.0 / NEIGH), update0 * (1.0 / NEIGH),
+    )
+    for at, matrix in enumerate(factors):
+        dense[at] = split_left(matrix)
 
 
 def lane_pick(table, lanes):
@@ -99,24 +105,26 @@
 
 
 def product(left, x):
-    rows = left.shape[0] // 2
-    hi, lo = halves(x)
-    both = jnp.dot(left, jnp.concatenate([hi, lo], axis=0).astype(bf16), preferred_element_type=f32)
-    return both[:rows] + both[rows:]
+    hi, lo = parts(x)
+    return jnp.dot(left, jnp.concatenate([hi, lo, hi], axis=0), preferred_element_type=f32)
 
 
 def sum_to(values, hot):
-    hi, lo = halves(values)
+    hi, lo = parts(values)
     both = lax.dot_general(
-        jnp.concatenate([hi, lo], axis=0).astype(bf16), hot, (((1,), (1,)), ((), ())), preferred_element_type=f32
+        jnp.concatenate([hi, lo], axis=0), hot, (((1,), (1,)), ((), ())), preferred_element_type=f32
     )
     return both[: values.shape[0]] + both[values.shape[0] :]
 
 
-def silu_and_slope(x):
-    s = 0.5 * jnp.tanh(0.5 * x) + 0.5
-    value = x * s
-    return value, s + value * (1.0 - s)
+def silu(h):
+    return h + h * jnp.tanh(h)
+
+
+def silu_and_slope(h):
+    t = jnp.tanh(h)
+    p = 1.0 + t
+    return h * p, p + p * (h - h * t)
 
 
 def sin_cos(x):
@@ -131,20 +139,29 @@
 
 def force_kernel(wx, wy, place, n_in, *refs):
     arrived = refs[:n_in]
-    geo, dense, radial_back, columns, out = refs[n_in : n_in + 5]
-    (raw, posb, lid_s, cl_s, spc, spn, unit, basis_s, slope_s, feats, sums, grads, pulls,
-     joined_s, lat_s, dpre_s, dz_s, back_s, total, tile_list, near_list) = refs[n_in + 5 :]
+    geo_in, dense_in, radial_back_in, columns_in, out = refs[n_in : n_in + 5]
+    (raw, posb, lid_s, cl_s, spc, spn, unit, basis_s, slope_s, feats2, sums, grads, pulls,
+     joined_s, lat_s, dpre_s, dz_s, back_s, total, tile_list, near_list,
+     geo, dense, radial_back, columns, sems) = refs[n_in + 5 :]
     tiles = 8
     n_dom = wx * wy
     nv = (wy + 1) // 2
     n_src = 3 * nv
     n_blk = wx * nv
-    width = feats.shape[1]
+    width = feats2.shape[1] // 2
     members = out.shape[0]
     own_a, own_b, slots = place()
 
-    for ref, at, slot in slots:
-        raw[slot] = arrived[ref][at * PACK_ROWS : (at + 1) * PACK_ROWS, :]
+    copies = [
+        pltpu.make_async_copy(arrived[ref].at[pl.ds(at * PACK_ROWS, PACK_ROWS), :], raw.at[slot], sems.at[k])
+        for k, (ref, at, slot) in enumerate(slots)
+    ]
+    loads = ((geo_in, geo), (dense_in, dense), (radial_back_in, radial_back), (columns_in, columns))
+    later = [pltpu.make_async_copy(src, dst, sems.at[n_dom + k]) for k, (src, dst) in enumerate(loads)]
+    for copy in copies + later:
+        copy.start()
+    for copy in copies:
+        copy.wait()
 
     none = n_dom * tiles
     count = jnp.int32(0)
@@ -287,6 +304,8 @@
         return carry
 
     chunks = lax.div(count + (CHUNK - 1), CHUNK)
+    for copy in later:
+        copy.wait()
     lax.fori_loop(0, chunks, forward, 0)
 
     sub = iota((8, LANES), 0)
@@ -295,7 +314,7 @@
         empty = jnp.zeros_like(kinds)
         rhs = jnp.concatenate([empty, empty, empty, kinds, kinds, empty], axis=0).astype(bf16)
         start = jnp.dot(geo[...], rhs, preferred_element_type=f32)[width:]
-        feats[k] = start + product(dense[6], sums[k])
+        feats2[k] = jnp.concatenate(parts(start + product(dense[6], sums[k])), axis=0)
 
     def middle(chunk, carry):
         taus = [tile_list[chunk * CHUNK + j] for j in range(CHUNK)]
@@ -304,23 +323,10 @@
             sources, home, half = spots(tau)
             lid = lid_s[pl.ds(tau, 1), :]
             clid = cl_s[pl.ds(tau, 1), :]
-            block = jnp.broadcast_to(lax.shift_right_arithmetic(lid, 7), (width, LANES))
-            value = None
-            for s in range(n_src):
-                picked = lane_pick(feats[sources[s]], lid & 127)
-                value = picked if value is None else jnp.where(block == s, picked, value)
-            joined.append(value + lane_pick(feats[home], clid & 127))
             lids.append((lid, clid - half * LANES))
             places.append((sources, home, half))
-        joined = side(joined)
-        latent = side([lat_s[tau] for tau in taus])
-        _, slope = silu_and_slope(product(dense[2], latent * joined))
-        dmix = product(dense[3], side([columns[1]] * CHUNK) * slope)
-        back = dmix * joined
-        spread = dmix * latent
+        hot_rows = []
         for j, tau in enumerate(taus):
-            cut = slice(j * LANES, (j + 1) * LANES)
-            back_s[tau] = back[:, cut]
             sources, home, half = places[j]
             lid, clid = lids[j]
             hots = [hot(lid - s * LANES) for s in range(n_src)]
@@ -328,7 +334,20 @@
             for v in range(nv):
                 here = own if nv == 1 else jnp.where(half == v, own, 0.0)
                 hots[nv + v] = hots[nv + v] + here
-            added = sum_to(spread[:, cut], jnp.concatenate(hots, axis=0).astype(bf16))
+            hot_rows.append(jnp.concatenate(hots, axis=0).astype(bf16))
+            both = jnp.dot(side([feats2[s] for s in sources]), hot_rows[-1], preferred_element_type=f32)
+            joined.append(both[:width] + both[width:])
+        joined = side(joined)
+        latent = side([lat_s[tau] for tau in taus])
+        _, slope = silu_and_slope(product(dense[2], latent * joined))
+        dmix = product(dense[3], slope)
+        back = dmix * joined
+        spread = dmix * latent
+        for j, tau in enumerate(taus):
+            cut = slice(j * LANES, (j + 1) * LANES)
+            back_s[tau] = back[:, cut]
+            sources, home, half = places[j]
+            added = sum_to(spread[:, cut], hot_rows[j])
             for s in range(n_src):
                 grads[sources[s]] += added[:, s * LANES : (s + 1) * LANES]
         return carry
@@ -336,7 +355,7 @@
     lax.fori_loop(0, chunks, middle, 0)
 
     for k in range(n_blk):
-        pulls[k] = product(dense[7], grads[k] + columns[0])
+        pulls[k] = product(dense[7], grads[k] + columns[...])
 
     own_block = own_a * nv + lax.div(own_b, 2)
 
@@ -391,26 +410,35 @@
     return lax.ppermute(value, axis, [(i, (i + by) % peers) for i in range(peers)])
 
 
-def swap(value, dx, dy):
-    nx, ny = lax.axis_size("gx"), lax.axis_size("gy")
-    pairs = [(a * ny + b, (a ^ dx) * ny + (b ^ dy)) for a in range(nx) for b in range(ny)]
-    return lax.ppermute(value, ("gx", "gy"), pairs)
+def swap(value, by_core):
+    sizes = [lax.axis_size(axis) for axis in ("gx", "gy", "gz")]
+    pairs = []
+    for a in range(sizes[0]):
+        for b in range(sizes[1]):
+            for c in range(sizes[2]):
+                dx, dy, dz = by_core[c]
+                pairs.append(((a * sizes[1] + b) * sizes[2] + c, ((a ^ dx) * sizes[1] + (b ^ dy)) * sizes[2] + (c ^ dz)))
+    return lax.ppermute(value, ("gx", "gy", "gz"), pairs)
 
 
 def gathered(own, gx, gy):
-    if gx == 4 and gy == 2:
-        pair = jnp.concatenate([own, swap(own, 2, 0)], axis=0)
-        arrays = [pair, swap(pair, 1, 0), swap(pair, 0, 1), swap(pair, 1, 1)]
+    if gx == 4 and gy == 2 and lax.axis_size("gz") == 2:
+        fetch = (((0, 1), (2, 1)), ((1, 0), (3, 0)), ((1, 1), (3, 1)))
+        far = swap(own, ((2, 0, 0), (2, 0, 0)))
+        fetched = [swap(own, (low + (0,), high + (0,))) for low, high in fetch]
+        handed = [swap(value, ((0, 0, 1), (0, 0, 1))) for value in fetched]
 
         def place():
-            a, b = lax.axis_index("gx"), lax.axis_index("gy")
-            slots = []
-            for k in range(4):
-                for at in range(2):
-                    slots.append((k, at, (a ^ ((k & 1) | (2 * at))) * 2 + (b ^ (k >> 1))))
+            a, b, c = lax.axis_index("gx"), lax.axis_index("gy"), lax.axis_index("gz")
+            slots = [(0, 0, a * 2 + b), (1, 0, (a ^ 2) * 2 + b)]
+            for k, (low, high) in enumerate(fetch):
+                mine = [jnp.where(c == 0, low[q], high[q]) for q in range(2)]
+                other = [jnp.where(c == 0, high[q], low[q]) for q in range(2)]
+                slots.append((2 + k, 0, (a ^ mine[0]) * 2 + (b ^ mine[1])))
+                slots.append((5 + k, 0, (a ^ other[0]) * 2 + (b ^ other[1])))
             return a, b, slots
 
-        return arrays, place
+        return [own, far] + fetched + handed, place
     wx, wy = window(gx), window(gy)
     steps = list(range(wy // 2 + 1)) + list(range(wy // 2 + 1 - wy, 0))
     column = jnp.concatenate([own if s == 0 else shift(own, "gy", -s) for s in steps], axis=0)
@@ -438,9 +466,9 @@
         weights_kernel,
         out_shape=(
             jax.ShapeDtypeStruct((2 * width, 48), bf16),
-            jax.ShapeDtypeStruct((8, 2 * width, 2 * width), bf16),
-            jax.ShapeDtypeStruct((2 * members * 8, 2 * width), bf16),
-            jax.ShapeDtypeStruct((2, width, LANES), f32),
+            jax.ShapeDtypeStruct((8, width, 3 * width), bf16),
+            jax.ShapeDtypeStruct((members * 8, 3 * width), bf16),
+            jax.ShapeDtypeStruct((width, LANES), f32),
         ),
         name="weights",
     )(embed, radial, w_mix, w_latent, w_update, readout)
@@ -449,6 +477,7 @@
     n_dom = wx * wy
     n_tiles = n_dom * 8
     n_blk = wx * ((wy + 1) // 2)
+    held = 5 * (n_tiles + 1) * width * LANES * 4 + 8 * 1024 * 1024
     per_tile = pltpu.VMEM((n_tiles + 1, width, LANES), f32)
     per_block = pltpu.VMEM((n_blk, width, LANES), f32)
     row_ids = pltpu.VMEM((n_tiles + 8, LANES), i32)
@@ -469,7 +498,7 @@
             pltpu.VMEM((3, n_tiles + 8, LANES), f32),
             pltpu.VMEM((n_tiles * 8 + 8, LANES), f32),
             pltpu.VMEM((n_tiles * 8 + 8, LANES), f32),
-            per_block,
+            pltpu.VMEM((n_blk, 2 * width, LANES), bf16),
             per_block,
             per_block,
             per_block,
@@ -481,8 +510,11 @@
             pltpu.VMEM((8, LANES), f32),
             pltpu.SMEM((n_tiles + 2 * CHUNK,), i32),
             pltpu.SMEM((n_tiles + 2 * CHUNK,), i32),
-        ],
-        compiler_params=pltpu.CompilerParams(vmem_limit_bytes=56 * 1024 * 1024),
+        ]
+        + [pltpu.VMEM(part.shape, part.dtype) for part in parts]
+        + [pltpu.SemaphoreType.DMA((n_dom + len(parts),))],
+        in_specs=[pl.BlockSpec(memory_space=pl.ANY)] * (len(arrays) + len(parts)),
+        compiler_params=pltpu.CompilerParams(vmem_limit_bytes=held),
         name="forces",
     )(*arrays, *parts)
 

time: 35.4 us -> 36.5 us (1.031)
  the two profiles are of different devices: /device:TPU:0 before, /device:TPU:5 now
where the time goes in v2:
time: 36.5 us; the launch traced here: 36.9 us
  Pallas kernels  23.8 us (65%)
  starting transfers between devices  7.04 us (19%)
  local copies, waits for them, and re-layouts  3.76 us (10%)
  waiting for transfers between devices  2.29 us (6%)
    pallas_call x1, Pallas kernels, on_device(): pl.pallas_call(body, out_shape=jax.ShapeDtypeStruct((members, 3, 1, 1, at...  20.3 us
    ppermute x7, starting transfers between devices, swap(): return lax.ppermute(value, ('gx', 'gy', 'gz'), pairs)  7.04 us
    unnamed x13, local copies, waits for them, and re-layouts  3.76 us
    ppermute x7, waiting for transfers between devices, swap(): return lax.ppermute(value, ('gx', 'gy', 'gz'), pairs)  2.29 us
    pallas_call x1, Pallas kernels, on_device(): pl.pallas_call(weights_kernel, out_shape=(jax.ShapeDtypeStruct((2 * width...  2.08 us
    pallas_call x1, Pallas kernels, on_device(): pl.pallas_call(pack_kernel, out_shape=jax.ShapeDtypeStruct((PACK_ROWS, LA...  1.43 us
  transfers between devices with their start and end apart: 7, of which 2 were waited for; matrix products, arithmetic and copies ran while one was open for 2% of the time, Pallas kernels for 6%

profile of v2, /device:TPU:5, one launch (start us, length us, event | category | flops | bytes accessed | tf_op | source)
XLA Modules:
  0.0 36.9 jit_solution(7353295531686402357)
XLA Ops:
  0.0 0.0 copy-start.5
  0.0 1.4 %pack.1.refs_0_ = f32[24,128]{1,0:T(8,128)} custom-call(f32[3,1,1,64]{3,2,1,0:T(1,128)} %pos.1, s32[1,1,64]{2,1,0:T(1,128)} %species.1, s32[1,1,1024]{2,1,0:T(1,128)} %centers.1, s32[1,1,1024]{2,1,0:T(1,128)} %neighbours.1, s32[1,1,1024]{2,1,0:T(1,128)} %masks.1, s32[1,1,32]{2,1,0:T(1,128)} %skin.1), custom_call_target="tpu_custom_call" | custom-call | tf_op jit(solution)/shard_map/pack/pallas_call | solution.py:462
  1.4 4.2 %collective-permute-start.3 = (f32[24,128]{1,0:T(8,128)}, f32[24,128]{1,0:T(8,128)S(1)}, u32[]{:S(2)}, u32[]{:S(2)}) collective-permute-start(f32[24,128]{1,0:T(8,128)} %pack.1.refs_0_), channel_id=1, source_target_pairs={{0,6},{1,15},{2,4},{3,13},{4,2},{5,11},{6,0},{7,9},{8,14},{9,7},{1... | collective-permute-start | bytes 36872 | tf_op jit(solution)/shard_map/ppermute | solution.py:421
  5.7 0.0 collective-permute-start.2
  5.7 0.4 %collective-permute-start.1 = (f32[24,128]{1,0:T(8,128)}, f32[24,128]{1,0:T(8,128)S(1)}, u32[]{:S(2)}, u32[]{:S(2)}) collective-permute-start(f32[24,128]{1,0:T(8,128)} %pack.1.refs_0_), channel_id=1, source_target_pairs={{0,2},{1,11},{2,0},{3,9},{4,6},{5,15},{6,4},{7,13},{8,10},{9,3},{1... | collective-permute-start | bytes 36872 | tf_op jit(solution)/shard_map/ppermute | solution.py:421
  6.1 1.9 %collective-permute-start = (f32[24,128]{1,0:T(8,128)}, f32[24,128]{1,0:T(8,128)S(1)}, u32[]{:S(2)}, u32[]{:S(2)}) collective-permute-start(f32[24,128]{1,0:T(8,128)} %pack.1.refs_0_), channel_id=1, source_target_pairs={{0,8},{1,9},{2,10},{3,11},{4,12},{5,13},{6,14},{7,15},{8,0},{9,1},... | collective-permute-start | bytes 36872 | tf_op jit(solution)/shard_map/ppermute | solution.py:421
  8.1 0.0 collective-permute-done.3.refs_4_
  8.1 0.1 collective-permute-start.6
  8.2 2.0 %collective-permute-done.2.refs_3_ = f32[24,128]{1,0:T(8,128)S(1)} collective-permute-done((f32[24,128]{1,0:T(8,128)}, f32[24,128]{1,0:T(8,128)S(1)}, u32[]{:S(2)}, u32[]{:S(2)}) %collective-permute-start.2) | collective-permute-done | bytes 12320 | tf_op jit(solution)/shard_map/ppermute | solution.py:421
  10.2 0.0 collective-permute-start.5
  10.2 0.2 collective-permute-done.1.refs_2_
  10.5 0.3 collective-permute-start.4
  10.8 0.0 copy-done.5
  10.8 0.6 %copy.13.embed = f32[2,5,32]{2,1,0:T(8,128)} copy(f32[2,5,32]{2,0,1:T(2,128)S(1)} %copy-done.5) | data formatting | bytes 2560 | tf_op args[6]
  11.4 0.0 copy-start.1
  11.4 2.1 %weights.1 = (bf16[128,48]{1,0:T(8,128)(2,1)}, bf16[8,64,192]{2,1,0:T(8,128)(2,1)}, bf16[16,192]{1,0:T(8,128)(2,1)}, f32[64,128]{1,0:T(8,128)}) custom-call(f32[2,5,32]{2,1,0:T(8,128)} %copy.13.embed, f32[2,8,32]{2,1,0:T(8,128)} %radial.1, f32[2,2,32,32]{3,2,1,0:T(8,128)} %w_mix.1, f32[2,1,32,32]{3,2,1,0:T(8,128)} %w_latent.1, f32[2,2,32,32]{3,2,1,0:T(8,128)} %w_update.1, ...), custom_call_target="tpu_custom_call" | custom-call | tf_op jit(solution)/shard_map/weights/pallas_call | solution.py:465
  13.4 0.0 collective-permute-done.refs_1_
  13.4 0.0 collective-permute-done.6.refs_7_
  13.4 0.0 collective-permute-done.5.refs_6_
  13.5 0.0 collective-permute-done.4.refs_5_
  13.5 0.0 copy-done.1
  13.5 0.0 copy-start
  13.5 0.9 %copy-done = bf16[8,64,192]{2,1,0:T(8,128)(2,1)S(1)} copy-done((bf16[8,64,192]{2,1,0:T(8,128)(2,1)S(1)}, bf16[8,64,192]{2,1,0:T(8,128)(2,1)}, u32[]{:S(2)}) %copy-start) | copy-done | bytes 196632
  14.4 0.0 copy-start.2
  14.4 0.8 %copy-done.2 = bf16[128,48]{1,0:T(8,128)(2,1)S(1)} copy-done((bf16[128,48]{1,0:T(8,128)(2,1)S(1)}, bf16[128,48]{1,0:T(8,128)(2,1)}, u32[]{:S(2)}) %copy-start.2) | copy-done | bytes 12312
  15.2 0.0 copy-start.3
  15.2 0.8 %copy-done.3 = f32[64,128]{1,0:T(8,128)S(1)} copy-done((f32[64,128]{1,0:T(8,128)S(1)}, f32[64,128]{1,0:T(8,128)}, u32[]{:S(2)}) %copy-start.3) | copy-done | bytes 32792
  15.9 0.0 copy-start.4
  15.9 0.7 %copy-done.4 = bf16[16,192]{1,0:T(8,128)(2,1)S(1)} copy-done((bf16[16,192]{1,0:T(8,128)(2,1)S(1)}, bf16[16,192]{1,0:T(8,128)(2,1)}, u32[]{:S(2)}) %copy-start.4) | copy-done | bytes 6168
  16.6 20.3 %forces.1 = f32[2,3,1,1,64]{4,3,2,1,0:T(1,128)} custom-call(f32[24,128]{1,0:T(8,128)S(1)} %copy-done.1, f32[24,128]{1,0:T(8,128)S(1)} %collective-permute-done.refs_1_, f32[24,128]{1,0:T(8,128)S(1)} %collective-permute-done.1.refs_2_, f32[24,128]{1,0:T(8,128)S(1)} %collective-permute-done.2.refs_3_, f32[24,128]{1,0:T(8,128)S(1)} %collective-permute-done.3.refs_4_, ...), custom_call_target="tpu_custom_call" | custom-call | tf_op jit(solution)/shard_map/forces/pallas_call | solution.py:488
Async XLA Ops:
  0.0 10.8 %copy-start.5 = (f32[2,5,32]{2,0,1:T(2,128)S(1)}, f32[2,5,32]{2,0,1:T(2,128)}, u32[]{:S(2)}) copy-start(f32[2,5,32]{2,0,1:T(2,128)} %param.18) | copy-start | bytes 3844
  1.4 6.6 %collective-permute-start.3 = (f32[24,128]{1,0:T(8,128)}, f32[24,128]{1,0:T(8,128)S(1)}, u32[]{:S(2)}, u32[]{:S(2)}) collective-permute-start(f32[24,128]{1,0:T(8,128)} %pack.1.refs_0_), channel_id=1, source_target_pairs={{0,6},{1,15},{2,4},{3,13},{4,2},{5,11},{6,0},{7,9},{8,14},{9,7},{1... | collective-permute-start | bytes 36872 | tf_op jit(solution)/shard_map/ppermute | solution.py:421
  5.7 4.6 %collective-permute-start.2 = (f32[24,128]{1,0:T(8,128)}, f32[24,128]{1,0:T(8,128)S(1)}, u32[]{:S(2)}, u32[]{:S(2)}) collective-permute-start(f32[24,128]{1,0:T(8,128)} %pack.1.refs_0_), channel_id=1, source_target_pairs={{0,4},{1,13},{2,6},{3,15},{4,0},{5,9},{6,2},{7,11},{8,12},{9,5},{1... | collective-permute-start | bytes 36872 | tf_op jit(solution)/shard_map/ppermute | solution.py:421
  5.7 4.8 %collective-permute-start.1 = (f32[24,128]{1,0:T(8,128)}, f32[24,128]{1,0:T(8,128)S(1)}, u32[]{:S(2)}, u32[]{:S(2)}) collective-permute-start(f32[24,128]{1,0:T(8,128)} %pack.1.refs_0_), channel_id=1, source_target_pairs={{0,2},{1,11},{2,0},{3,9},{4,6},{5,15},{6,4},{7,13},{8,10},{9,3},{1... | collective-permute-start | bytes 36872 | tf_op jit(solution)/shard_map/ppermute | solution.py:421
  6.1 7.3 %collective-permute-start = (f32[24,128]{1,0:T(8,128)}, f32[24,128]{1,0:T(8,128)S(1)}, u32[]{:S(2)}, u32[]{:S(2)}) collective-permute-start(f32[24,128]{1,0:T(8,128)} %pack.1.refs_0_), channel_id=1, source_target_pairs={{0,8},{1,9},{2,10},{3,11},{4,12},{5,13},{6,14},{7,15},{8,0},{9,1},... | collective-permute-start | bytes 36872 | tf_op jit(solution)/shard_map/ppermute | solution.py:421
  8.1 5.4 %collective-permute-start.6 = (f32[24,128]{1,0:T(8,128)S(1)}, f32[24,128]{1,0:T(8,128)S(1)}, u32[]{:S(2)}, u32[]{:S(2)}) collective-permute-start(f32[24,128]{1,0:T(8,128)S(1)} %collective-permute-done.3.refs_4_), channel_id=1, source_target_pairs={{0,1},{1,0},{2,3},{3,2},{4,5},{5,4},{6,7},{7,6},{8,9},{9,8},{10,11... | collective-permute-start | bytes 36872 | tf_op jit(solution)/shard_map/ppermute | solution.py:421
  10.2 3.2 %collective-permute-start.5 = (f32[24,128]{1,0:T(8,128)S(1)}, f32[24,128]{1,0:T(8,128)S(1)}, u32[]{:S(2)}, u32[]{:S(2)}) collective-permute-start(f32[24,128]{1,0:T(8,128)S(1)} %collective-permute-done.2.refs_3_), channel_id=1, source_target_pairs={{0,1},{1,0},{2,3},{3,2},{4,5},{5,4},{6,7},{7,6},{8,9},{9,8},{10,11... | collective-permute-start | bytes 36872 | tf_op jit(solution)/shard_map/ppermute | solution.py:421
  10.5 3.0 %collective-permute-start.4 = (f32[24,128]{1,0:T(8,128)S(1)}, f32[24,128]{1,0:T(8,128)S(1)}, u32[]{:S(2)}, u32[]{:S(2)}) collective-permute-start(f32[24,128]{1,0:T(8,128)S(1)} %collective-permute-done.1.refs_2_), channel_id=1, source_target_pairs={{0,1},{1,0},{2,3},{3,2},{4,5},{5,4},{6,7},{7,6},{8,9},{9,8},{10,11... | collective-permute-start | bytes 36872 | tf_op jit(solution)/shard_map/ppermute | solution.py:421
  11.4 2.1 %copy-start.1 = (f32[24,128]{1,0:T(8,128)S(1)}, f32[24,128]{1,0:T(8,128)}, u32[]{:S(2)}) copy-start(f32[24,128]{1,0:T(8,128)} %pack.1.refs_0_) | copy-start | bytes 36868
  13.5 1.0 %copy-start = (bf16[8,64,192]{2,1,0:T(8,128)(2,1)S(1)}, bf16[8,64,192]{2,1,0:T(8,128)(2,1)}, u32[]{:S(2)}) copy-start(bf16[8,64,192]{2,1,0:T(8,128)(2,1)} %get-tuple-element.10.refs_9_) | copy-start | bytes 589828
  14.4 0.8 %copy-start.2 = (bf16[128,48]{1,0:T(8,128)(2,1)S(1)}, bf16[128,48]{1,0:T(8,128)(2,1)}, u32[]{:S(2)}) copy-start(bf16[128,48]{1,0:T(8,128)(2,1)} %get-tuple-element.9.refs_8_) | copy-start | bytes 36868
  15.2 0.8 %copy-start.3 = (f32[64,128]{1,0:T(8,128)S(1)}, f32[64,128]{1,0:T(8,128)}, u32[]{:S(2)}) copy-start(f32[64,128]{1,0:T(8,128)} %get-tuple-element.12.refs_11_) | copy-start | bytes 98308
  15.9 0.7 %copy-start.4 = (bf16[16,192]{1,0:T(8,128)(2,1)S(1)}, bf16[16,192]{1,0:T(8,128)(2,1)}, u32[]{:S(2)}) copy-start(bf16[16,192]{1,0:T(8,128)(2,1)} %get-tuple-element.11.refs_10_) | copy-start | bytes 18436
